TPU v7x, 32 devices: a whole 2x2x4 slice. The times are simulated.
32 devices in a mesh: ctx: 8 (over z, y), tp: 4 (over x, core).
Axes of the slice: x: 2, y: 2, z: 4, core: 2. Of those that a mesh axis runs over, the one named last changes fastest.
Arguments:
- streams: bfloat16 [3, 256, 1024], P(None, 'tp', 'ctx'), may hold values from -6 to 6
- filter_raw: float32 [256, 1024], P('tp', 'ctx'), may hold values from -6 to 6
- grad_output: bfloat16 [256, 1024], P('tp', 'ctx'), may hold values from -6 to 6
Outputs:
- mixed_out: bfloat16 [256, 1024], P('tp', 'ctx')
- grad_streams: bfloat16 [3, 256, 1024], P(None, 'tp', 'ctx')
- grad_filter: float32 [256, 1024], P('tp', 'ctx')
All inputs are finite; a program needn't handle non-finite values.
Results may differ from a plain program's by a relative error of at most 0.0014.
Values sent between devices are 32-bit elements; how exact they have to be, the bound alone decides.
No kernel may reach another device: no remote copies, remote signals or barrier semaphores. Data moves between devices by JAX's collectives and lax.ppermute only.
A program may use at most 64 MiB of HBM per device.

v0:
```python
import math

import jax
import jax.numpy as jnp
from jax import lax
from jax.sharding import PartitionSpec as P

highest = lax.Precision.HIGHEST


def dft_tables(slow, fast, devices, position):
    length = slow * fast
    stride = fast // devices
    freq_slow = jnp.arange(slow, dtype=jnp.int32)
    rows_slow = jnp.arange(devices, dtype=jnp.int32)
    angle_slow = (
        2.0 * math.pi / slow * (freq_slow[:, None] * rows_slow[None, :] % slow).astype(jnp.float32)
    )
    cols_twist = position * stride + jnp.arange(stride, dtype=jnp.int32)
    angle_twist = (
        2.0
        * math.pi
        / length
        * (freq_slow[:, None] * cols_twist[None, :] % length).astype(jnp.float32)
    )
    freq_fast = jnp.arange(fast, dtype=jnp.int32)
    angle_fast = (
        2.0 * math.pi / fast * (freq_fast[:, None] * freq_fast[None, :] % fast).astype(jnp.float32)
    )
    return (
        jnp.cos(angle_slow),
        jnp.sin(angle_slow),
        jnp.cos(angle_twist)[:, None, :],
        jnp.sin(angle_twist)[:, None, :],
        jnp.cos(angle_fast),
        jnp.sin(angle_fast),
    )


def forward_spectrum(signal, tables):
    cos_slow, sin_slow, cos_twist, sin_twist, cos_fast, sin_fast = tables
    stacked, channels, fast = signal.shape
    slow, devices = cos_slow.shape
    stride = fast // devices
    columns = lax.all_to_all(signal[:, None], "ctx", split_axis=3, concat_axis=1, tiled=True)
    flat = columns.reshape(stacked, devices, channels * stride)
    real_part = jnp.einsum("ka,sam->skm", cos_slow, flat, precision=highest).reshape(
        stacked, slow, channels, stride
    )
    imag_part = -jnp.einsum("ka,sam->skm", sin_slow, flat, precision=highest).reshape(
        stacked, slow, channels, stride
    )
    turned_real = real_part * cos_twist + imag_part * sin_twist
    turned_imag = imag_part * cos_twist - real_part * sin_twist
    rows_real, rows_imag = (
        lax.all_to_all(turned_real, "ctx", split_axis=1, concat_axis=3, tiled=True),
        lax.all_to_all(turned_imag, "ctx", split_axis=1, concat_axis=3, tiled=True),
    )
    spec_real = jnp.matmul(rows_real, cos_fast, precision=highest) + jnp.matmul(
        rows_imag, sin_fast, precision=highest
    )
    spec_imag = jnp.matmul(rows_imag, cos_fast, precision=highest) - jnp.matmul(
        rows_real, sin_fast, precision=highest
    )
    return (spec_real, spec_imag)


def inverse_signal(spec_real, spec_imag, tables):
    cos_slow, sin_slow, cos_twist, sin_twist, cos_fast, sin_fast = tables
    stacked, local_rows, channels, fast = spec_real.shape
    slow, devices = cos_slow.shape
    stride = fast // devices
    back_real = jnp.matmul(spec_real, cos_fast, precision=highest) - jnp.matmul(
        spec_imag, sin_fast, precision=highest
    )
    back_imag = jnp.matmul(spec_imag, cos_fast, precision=highest) + jnp.matmul(
        spec_real, sin_fast, precision=highest
    )
    cols_real, cols_imag = (
        lax.all_to_all(back_real, "ctx", split_axis=3, concat_axis=1, tiled=True),
        lax.all_to_all(back_imag, "ctx", split_axis=3, concat_axis=1, tiled=True),
    )
    turned_real = (cols_real * cos_twist - cols_imag * sin_twist).reshape(
        stacked, slow, channels * stride
    )
    turned_imag = (cols_imag * cos_twist + cols_real * sin_twist).reshape(
        stacked, slow, channels * stride
    )
    timeline = jnp.einsum("ka,skm->sam", cos_slow, turned_real, precision=highest) - jnp.einsum(
        "ka,skm->sam", sin_slow, turned_imag, precision=highest
    )
    timeline = timeline.reshape(stacked, devices, channels, stride)
    returned = lax.all_to_all(timeline, "ctx", split_axis=1, concat_axis=3, tiled=True)
    return returned[:, 0] / float(slow * fast)


def conv_product(gated_real, gated_imag, taps_real, taps_imag):
    conv_real = gated_real * taps_real - gated_imag * taps_imag
    conv_imag = gated_real * taps_imag + gated_imag * taps_real
    return (conv_real, conv_imag)


def corr_products(grad_real, grad_imag, gated_real, gated_imag, taps_real, taps_imag):
    corr_real = jnp.stack(
        [
            grad_real * taps_real + grad_imag * taps_imag,
            grad_real * gated_real + grad_imag * gated_imag,
        ]
    )
    corr_imag = jnp.stack(
        [
            grad_imag * taps_real - grad_real * taps_imag,
            grad_imag * gated_real - grad_real * gated_imag,
        ]
    )
    return (corr_real, corr_imag)


def local(streams, filter_raw, grad_output):
    devices = lax.axis_size("ctx")
    position = lax.axis_index("ctx")
    channels, fast = filter_raw.shape
    slow = 2 * devices
    tap_scale = 1.0 / math.sqrt(fast * devices)
    tables = dft_tables(slow, fast, devices, position)
    query_part = streams[0].astype(jnp.float32)
    key_part = streams[1].astype(jnp.float32)
    value_part = streams[2].astype(jnp.float32)
    gated_input = key_part * value_part
    kernel_taps = filter_raw * tap_scale
    upstream = grad_output.astype(jnp.float32)
    grad_conv = query_part * upstream
    spec_real, spec_imag = forward_spectrum(jnp.stack([gated_input, kernel_taps]), tables)
    conv_real, conv_imag = conv_product(spec_real[0], spec_imag[0], spec_real[1], spec_imag[1])
    long_conv = inverse_signal(conv_real[None], conv_imag[None], tables)[0]
    grad_real, grad_imag = forward_spectrum(grad_conv[None], tables)
    corr_real, corr_imag = corr_products(
        grad_real[0], grad_imag[0], spec_real[0], spec_imag[0], spec_real[1], spec_imag[1]
    )
    both_back = inverse_signal(corr_real, corr_imag, tables)
    grad_gated = both_back[0]
    filter_back = both_back[1]
    grad_filter = filter_back * tap_scale
    mixed_out = (query_part * long_conv).astype(jnp.bfloat16)
    grad_query = (upstream * long_conv).astype(jnp.bfloat16)
    grad_key = (grad_gated * value_part).astype(jnp.bfloat16)
    grad_value = (grad_gated * key_part).astype(jnp.bfloat16)
    grad_streams = jnp.stack([grad_query, grad_key, grad_value], axis=0)
    return (mixed_out, grad_streams, grad_filter)


def solution(mesh):
    in_specs = (P(None, "tp", "ctx"), P("tp", "ctx"), P("tp", "ctx"))
    out_specs = (P("tp", "ctx"), P(None, "tp", "ctx"), P("tp", "ctx"))
    return jax.shard_map(local, mesh=mesh, in_specs=in_specs, out_specs=out_specs, check_vma=False)
```

profile of v0, /device:TPU:0, one launch (start us, length us, event | category | flops | bytes accessed | tf_op | source)
XLA Modules:
  0.0 150.8 jit_solution(7924482140615578857)
XLA Ops:
  0.6 0.8 fusion.210
  1.5 0.6 copy-done.1
  2.2 0.5 broadcast.226
  2.8 0.8 reduce
  3.6 0.7 reshape.254
  4.3 7.3 %all-to-all-start.6 = ((f32[8,1,1024]{2,1,0:T(1,128)}), f32[8,1,1024]{2,1,0:T(1,128)S(1)}, u32[]{:S(2)}, u32[]{:S(2)}) async-start(f32[8,1,1024]{2,1,0:T(1,128)} %reshape.254), calls=%async_computation.6 | async-start | bytes 65536 | tf_op jit(solution)/shard_map/all_to_all | solution.py:45
  11.9 0.6 copy-done
  12.8 0.8 reshape.242
  14.2 4.1 %all-to-all-done.6 = f32[8,1,1024]{2,1,0:T(1,128)S(1)} async-done(((f32[8,1,1024]{2,1,0:T(1,128)}), f32[8,1,1024]{2,1,0:T(1,128)S(1)}, u32[]{:S(2)}, u32[]{:S(2)}) %all-to-all-start.6) | async-done | bytes 32800 | tf_op jit(solution)/shard_map/all_to_all | solution.py:45
  18.3 3.3 %all-to-all-start = ((f32[8,1,2048]{2,1,0:T(1,128)}), f32[8,1,2048]{2,1,0:T(1,128)S(1)}, u32[]{:S(2)}, u32[]{:S(2)}) async-start(f32[8,1,2048]{2,1,0:T(1,128)} %reshape.242), calls=%async_computation | async-start | bytes 131072 | tf_op jit(solution)/shard_map/all_to_all | solution.py:45
  21.6 0.7 reduce.1
  24.2 0.8 reshape.256
  25.1 0.8 reshape.258
  25.8 2.6 %all-to-all-done = f32[8,1,2048]{2,1,0:T(1,128)S(1)} async-done(((f32[8,1,2048]{2,1,0:T(1,128)}), f32[8,1,2048]{2,1,0:T(1,128)S(1)}, u32[]{:S(2)}, u32[]{:S(2)}) %all-to-all-start) | async-done | bytes 65568 | tf_op jit(solution)/shard_map/all_to_all | solution.py:45
  28.5 3.3 %all-to-all-start.7 = ((f32[8,1,2048]{2,1,0:T(1,128)}), f32[8,1,2048]{2,1,0:T(1,128)S(1)}, u32[]{:S(2)}, u32[]{:S(2)}) async-start(f32[8,1,2048]{2,1,0:T(1,128)} %reshape.256), calls=%async_computation.7 | async-start | bytes 131072 | tf_op jit(solution)/shard_map/all_to_all | solution.py:56
  31.8 0.8 reduce.4
  34.4 1.4 reshape.226
  35.7 1.6 %multiply_add_fusion = (f32[2,16,64,16]{3,2,1,0:T(8,128)S(1)}, f32[2,16,64,16]{3,2,1,0:T(8,128)S(1)}) fusion(f32[2,16,64,16]{3,2,1,0:T(8,128)S(1)} %neg.35, f32[2,16,64,16]{3,2,1,0:T(8,128)} %reshape.226, f32[16,16]{1,0:T(8,128)S(1)} %get-tuple-element.29, f32[16,16]{1,0:T(8,128)S(1)} %get-tuple-element.28), kind=kLoop, calls=%fused_computation.23 | loop fusion | flops 196608 | bytes 526336 | tf_op jit(solution)/shard_map/add | solution.py:53
  37.6 0.8 reshape.246
  38.8 0.8 reshape.244
  39.6 6.0 %all-to-all-start.8 = ((f32[8,1,2048]{2,1,0:T(1,128)}), f32[8,1,2048]{2,1,0:T(1,128)S(1)}, u32[]{:S(2)}, u32[]{:S(2)}) async-start(f32[8,1,2048]{2,1,0:T(1,128)} %reshape.258), calls=%async_computation.8 | async-start | bytes 131072 | tf_op jit(solution)/shard_map/all_to_all | solution.py:57
  45.6 0.8 reduce.2
  46.9 5.5 %all-to-all-done.8 = f32[8,1,2048]{2,1,0:T(1,128)S(1)} async-done(((f32[8,1,2048]{2,1,0:T(1,128)}), f32[8,1,2048]{2,1,0:T(1,128)S(1)}, u32[]{:S(2)}, u32[]{:S(2)}) %all-to-all-start.8) | async-done | bytes 65568 | tf_op jit(solution)/shard_map/all_to_all | solution.py:57
  52.5 3.4 %all-to-all-start.1 = ((f32[8,1,4096]{2,1,0:T(1,128)}), f32[8,1,4096]{2,1,0:T(1,128)S(1)}, u32[]{:S(2)}, u32[]{:S(2)}) async-start(f32[8,1,4096]{2,1,0:T(1,128)} %reshape.246), calls=%async_computation.1 | async-start | bytes 262144 | tf_op jit(solution)/shard_map/all_to_all | solution.py:56
  55.9 0.8 reduce.3
  57.7 5.4 %all-to-all-done.1 = f32[8,1,4096]{2,1,0:T(1,128)S(1)} async-done(((f32[8,1,4096]{2,1,0:T(1,128)}), f32[8,1,4096]{2,1,0:T(1,128)S(1)}, u32[]{:S(2)}, u32[]{:S(2)}) %all-to-all-start.1) | async-done | bytes 131104 | tf_op jit(solution)/shard_map/all_to_all | solution.py:56
  63.1 3.6 %all-to-all-start.2 = ((f32[8,1,4096]{2,1,0:T(1,128)}), f32[8,1,4096]{2,1,0:T(1,128)S(1)}, u32[]{:S(2)}, u32[]{:S(2)}) async-start(f32[8,1,4096]{2,1,0:T(1,128)} %reshape.244), calls=%async_computation.2 | async-start | bytes 262144 | tf_op jit(solution)/shard_map/all_to_all | solution.py:57
  66.7 1.0 reduce.6
  67.8 0.6 fusion.48
  68.4 5.4 %all-to-all-done.2 = f32[8,1,4096]{2,1,0:T(1,128)S(1)} async-done(((f32[8,1,4096]{2,1,0:T(1,128)}), f32[8,1,4096]{2,1,0:T(1,128)S(1)}, u32[]{:S(2)}, u32[]{:S(2)}) %all-to-all-start.2) | async-done | bytes 131104 | tf_op jit(solution)/shard_map/all_to_all | solution.py:57
  73.8 1.0 reduce.5
  74.9 0.6 fusion.46
  75.5 0.6 convolution_add_fusion.1
  76.1 0.6 convolution_subtract_fusion.1
  78.7 0.8 reshape.250
  79.5 3.3 %all-to-all-start.3 = ((f32[8,1,2048]{2,1,0:T(1,128)}), f32[8,1,2048]{2,1,0:T(1,128)S(1)}, u32[]{:S(2)}, u32[]{:S(2)}) async-start(f32[8,1,2048]{2,1,0:T(1,128)} %reshape.250), calls=%async_computation.3 | async-start | bytes 131072 | tf_op jit(solution)/shard_map/all_to_all | solution.py:80
  83.4 0.8 reshape.248
  84.7 5.0 %all-to-all-done.3 = f32[8,1,2048]{2,1,0:T(1,128)S(1)} async-done(((f32[8,1,2048]{2,1,0:T(1,128)}), f32[8,1,2048]{2,1,0:T(1,128)S(1)}, u32[]{:S(2)}, u32[]{:S(2)}) %all-to-all-start.3) | async-done | bytes 65568 | tf_op jit(solution)/shard_map/all_to_all | solution.py:80
  89.7 3.3 %all-to-all-start.4 = ((f32[8,1,2048]{2,1,0:T(1,128)}), f32[8,1,2048]{2,1,0:T(1,128)S(1)}, u32[]{:S(2)}, u32[]{:S(2)}) async-start(f32[8,1,2048]{2,1,0:T(1,128)} %reshape.248), calls=%async_computation.4 | async-start | bytes 131072 | tf_op jit(solution)/shard_map/all_to_all | solution.py:81
  93.0 0.5 convolution_subtract_fusion
  93.5 0.8 reduce.8
  95.0 4.9 %all-to-all-done.4 = f32[8,1,2048]{2,1,0:T(1,128)S(1)} async-done(((f32[8,1,2048]{2,1,0:T(1,128)}), f32[8,1,2048]{2,1,0:T(1,128)S(1)}, u32[]{:S(2)}, u32[]{:S(2)}) %all-to-all-start.4) | async-done | bytes 65568 | tf_op jit(solution)/shard_map/all_to_all | solution.py:81
  99.9 0.8 reduce.7
  102.0 0.7 reshape.252
  102.7 3.3 %all-to-all-start.5 = ((f32[8,1,1024]{2,1,0:T(1,128)}), f32[8,1,1024]{2,1,0:T(1,128)S(1)}, u32[]{:S(2)}, u32[]{:S(2)}) async-start(f32[8,1,1024]{2,1,0:T(1,128)} %reshape.252), calls=%async_computation.5 | async-start | bytes 65536 | tf_op jit(solution)/shard_map/all_to_all | solution.py:93
  106.8 0.9 reshape.262
  107.7 5.2 %all-to-all-done.5 = f32[8,1,1024]{2,1,0:T(1,128)S(1)} async-done(((f32[8,1,1024]{2,1,0:T(1,128)}), f32[8,1,1024]{2,1,0:T(1,128)S(1)}, u32[]{:S(2)}, u32[]{:S(2)}) %all-to-all-start.5) | async-done | bytes 32800 | tf_op jit(solution)/shard_map/all_to_all | solution.py:93
  112.9 3.4 %all-to-all-start.9 = ((f32[8,1,4096]{2,1,0:T(1,128)}), f32[8,1,4096]{2,1,0:T(1,128)S(1)}, u32[]{:S(2)}, u32[]{:S(2)}) async-start(f32[8,1,4096]{2,1,0:T(1,128)} %reshape.262), calls=%async_computation.9 | async-start | bytes 262144 | tf_op jit(solution)/shard_map/all_to_all | solution.py:80
  117.0 0.9 reshape.260
  117.9 5.9 %all-to-all-done.9 = f32[8,1,4096]{2,1,0:T(1,128)S(1)} async-done(((f32[8,1,4096]{2,1,0:T(1,128)}), f32[8,1,4096]{2,1,0:T(1,128)S(1)}, u32[]{:S(2)}, u32[]{:S(2)}) %all-to-all-start.9) | async-done | bytes 131104 | tf_op jit(solution)/shard_map/all_to_all | solution.py:80
  123.7 3.6 %all-to-all-start.10 = ((f32[8,1,4096]{2,1,0:T(1,128)}), f32[8,1,4096]{2,1,0:T(1,128)S(1)}, u32[]{:S(2)}, u32[]{:S(2)}) async-start(f32[8,1,4096]{2,1,0:T(1,128)} %reshape.260), calls=%async_computation.10 | async-start | bytes 262144 | tf_op jit(solution)/shard_map/all_to_all | solution.py:81
  127.3 0.7 reduce.9
  128.1 1.0 reduce.11
  129.7 0.6 all_to_all.168
  130.3 4.1 %all-to-all-done.10 = f32[8,1,4096]{2,1,0:T(1,128)S(1)} async-done(((f32[8,1,4096]{2,1,0:T(1,128)}), f32[8,1,4096]{2,1,0:T(1,128)S(1)}, u32[]{:S(2)}, u32[]{:S(2)}) %all-to-all-start.10) | async-done | bytes 131104 | tf_op jit(solution)/shard_map/all_to_all | solution.py:81
  134.4 1.0 reduce.10
  135.9 0.6 all_to_all.172
  137.5 0.8 reshape.264
  138.2 3.3 %all-to-all-start.11 = ((f32[8,1,2048]{2,1,0:T(1,128)}), f32[8,1,2048]{2,1,0:T(1,128)S(1)}, u32[]{:S(2)}, u32[]{:S(2)}) async-start(f32[8,1,2048]{2,1,0:T(1,128)} %reshape.264), calls=%async_computation.11 | async-start | bytes 131072 | tf_op jit(solution)/shard_map/all_to_all | solution.py:93
  141.6 0.7 copy.89
  142.3 6.1 %all-to-all-done.11 = f32[8,1,2048]{2,1,0:T(1,128)S(1)} async-done(((f32[8,1,2048]{2,1,0:T(1,128)}), f32[8,1,2048]{2,1,0:T(1,128)S(1)}, u32[]{:S(2)}, u32[]{:S(2)}) %all-to-all-start.11) | async-done | bytes 65568 | tf_op jit(solution)/shard_map/all_to_all | solution.py:93
  148.4 0.8 reduce.12
  149.4 0.7 copy.90
  150.1 0.7 copy.91
  (91 shorter events, 16.0 us)
Async XLA Ops:
  1.4 0.7 copy-start.1
  4.3 14.0 %all-to-all-start.6 = ((f32[8,1,1024]{2,1,0:T(1,128)}), f32[8,1,1024]{2,1,0:T(1,128)S(1)}, u32[]{:S(2)}, u32[]{:S(2)}) async-start(f32[8,1,1024]{2,1,0:T(1,128)} %reshape.254), calls=%async_computation.6 | async-start | bytes 65536 | tf_op jit(solution)/shard_map/all_to_all | solution.py:45
  11.8 0.8 copy-start
  18.3 10.2 %all-to-all-start = ((f32[8,1,2048]{2,1,0:T(1,128)}), f32[8,1,2048]{2,1,0:T(1,128)S(1)}, u32[]{:S(2)}, u32[]{:S(2)}) async-start(f32[8,1,2048]{2,1,0:T(1,128)} %reshape.242), calls=%async_computation | async-start | bytes 131072 | tf_op jit(solution)/shard_map/all_to_all | solution.py:45
  28.5 11.1 %all-to-all-start.7 = ((f32[8,1,2048]{2,1,0:T(1,128)}), f32[8,1,2048]{2,1,0:T(1,128)S(1)}, u32[]{:S(2)}, u32[]{:S(2)}) async-start(f32[8,1,2048]{2,1,0:T(1,128)} %reshape.256), calls=%async_computation.7 | async-start | bytes 131072 | tf_op jit(solution)/shard_map/all_to_all | solution.py:56
  39.6 12.9 %all-to-all-start.8 = ((f32[8,1,2048]{2,1,0:T(1,128)}), f32[8,1,2048]{2,1,0:T(1,128)S(1)}, u32[]{:S(2)}, u32[]{:S(2)}) async-start(f32[8,1,2048]{2,1,0:T(1,128)} %reshape.258), calls=%async_computation.8 | async-start | bytes 131072 | tf_op jit(solution)/shard_map/all_to_all | solution.py:57
  52.5 10.7 %all-to-all-start.1 = ((f32[8,1,4096]{2,1,0:T(1,128)}), f32[8,1,4096]{2,1,0:T(1,128)S(1)}, u32[]{:S(2)}, u32[]{:S(2)}) async-start(f32[8,1,4096]{2,1,0:T(1,128)} %reshape.246), calls=%async_computation.1 | async-start | bytes 262144 | tf_op jit(solution)/shard_map/all_to_all | solution.py:56
  63.1 10.7 %all-to-all-start.2 = ((f32[8,1,4096]{2,1,0:T(1,128)}), f32[8,1,4096]{2,1,0:T(1,128)S(1)}, u32[]{:S(2)}, u32[]{:S(2)}) async-start(f32[8,1,4096]{2,1,0:T(1,128)} %reshape.244), calls=%async_computation.2 | async-start | bytes 262144 | tf_op jit(solution)/shard_map/all_to_all | solution.py:57
  79.5 10.2 %all-to-all-start.3 = ((f32[8,1,2048]{2,1,0:T(1,128)}), f32[8,1,2048]{2,1,0:T(1,128)S(1)}, u32[]{:S(2)}, u32[]{:S(2)}) async-start(f32[8,1,2048]{2,1,0:T(1,128)} %reshape.250), calls=%async_computation.3 | async-start | bytes 131072 | tf_op jit(solution)/shard_map/all_to_all | solution.py:80
  89.7 10.2 %all-to-all-start.4 = ((f32[8,1,2048]{2,1,0:T(1,128)}), f32[8,1,2048]{2,1,0:T(1,128)S(1)}, u32[]{:S(2)}, u32[]{:S(2)}) async-start(f32[8,1,2048]{2,1,0:T(1,128)} %reshape.248), calls=%async_computation.4 | async-start | bytes 131072 | tf_op jit(solution)/shard_map/all_to_all | solution.py:81
  102.7 10.2 %all-to-all-start.5 = ((f32[8,1,1024]{2,1,0:T(1,128)}), f32[8,1,1024]{2,1,0:T(1,128)S(1)}, u32[]{:S(2)}, u32[]{:S(2)}) async-start(f32[8,1,1024]{2,1,0:T(1,128)} %reshape.252), calls=%async_computation.5 | async-start | bytes 65536 | tf_op jit(solution)/shard_map/all_to_all | solution.py:93
  112.9 10.9 %all-to-all-start.9 = ((f32[8,1,4096]{2,1,0:T(1,128)}), f32[8,1,4096]{2,1,0:T(1,128)S(1)}, u32[]{:S(2)}, u32[]{:S(2)}) async-start(f32[8,1,4096]{2,1,0:T(1,128)} %reshape.262), calls=%async_computation.9 | async-start | bytes 262144 | tf_op jit(solution)/shard_map/all_to_all | solution.py:80
  123.7 10.7 %all-to-all-start.10 = ((f32[8,1,4096]{2,1,0:T(1,128)}), f32[8,1,4096]{2,1,0:T(1,128)S(1)}, u32[]{:S(2)}, u32[]{:S(2)}) async-start(f32[8,1,4096]{2,1,0:T(1,128)} %reshape.260), calls=%async_computation.10 | async-start | bytes 262144 | tf_op jit(solution)/shard_map/all_to_all | solution.py:81
  138.2 10.2 %all-to-all-start.11 = ((f32[8,1,2048]{2,1,0:T(1,128)}), f32[8,1,2048]{2,1,0:T(1,128)S(1)}, u32[]{:S(2)}, u32[]{:S(2)}) async-start(f32[8,1,2048]{2,1,0:T(1,128)} %reshape.264), calls=%async_computation.11 | async-start | bytes 131072 | tf_op jit(solution)/shard_map/all_to_all | solution.py:93
where the time goes:
time: 152 us; the launch traced here: 151 us
  waiting for transfers between devices  54.2 us (36%)
  starting transfers between devices  47.2 us (31%)
  local copies, waits for them, and re-layouts  24.9 us (16%)
  other arithmetic  12.8 us (8%)
  matrix products  10.4 us (7%)
    unnamed x37, local copies, waits for them, and re-layouts  15.3 us
    all_to_all x2, waiting for transfers between devices, inverse_signal(): lax.all_to_all(timeline, 'ctx', split_axis=1, concat_axis=3, tiled=True)  11.3 us
    all_to_all x2, waiting for transfers between devices, forward_spectrum(): lax.all_to_all(turned_imag, 'ctx', split_axis=1, concat_axis=3, tiled=True)  10.9 us
    all_to_all x2, waiting for transfers between devices, inverse_signal(): lax.all_to_all(back_real, 'ctx', split_axis=3, concat_axis=1, tiled=True)  10.8 us
    all_to_all x2, starting transfers between devices, forward_spectrum(): lax.all_to_all(signal[:, None], 'ctx', split_axis=3, concat_axis=1, tiled...  10.6 us
    all_to_all x2, starting transfers between devices, forward_spectrum(): lax.all_to_all(turned_imag, 'ctx', split_axis=1, concat_axis=3, tiled=True)  9.51 us
    all_to_all x2, waiting for transfers between devices, inverse_signal(): lax.all_to_all(back_imag, 'ctx', split_axis=3, concat_axis=1, tiled=True)  8.95 us
    all_to_all x2, starting transfers between devices, inverse_signal(): lax.all_to_all(back_imag, 'ctx', split_axis=3, concat_axis=1, tiled=True)  6.94 us
  transfers between devices with their start and end apart: 12, of which 11 were waited for; matrix products, arithmetic and copies ran while one was open for 19% of the time, Pallas kernels for 0%

commit v1 on v0

--- a/solution.py
+++ b/solution.py
@@ -2,7 +2,10 @@
 
 import jax
 import jax.numpy as jnp
+import numpy as np
 from jax import lax
+from jax.experimental import pallas as pl
+from jax.experimental.pallas import tpu as pltpu
 from jax.sharding import PartitionSpec as P
 
 highest = lax.Precision.HIGHEST
@@ -116,7 +119,7 @@
     return (corr_real, corr_imag)
 
 
-def local(streams, filter_raw, grad_output):
+def by_residue(streams, filter_raw, grad_output):
     devices = lax.axis_size("ctx")
     position = lax.axis_index("ctx")
     channels, fast = filter_raw.shape
@@ -149,6 +152,206 @@
     return (mixed_out, grad_streams, grad_filter)
 
 
+def table(angle):
+    return np.cos(angle), np.sin(angle)
+
+
+def circle(count, at):
+    exact = {0: (1.0, 0.0), 1: (0.0, 1.0), 2: (-1.0, 0.0), 3: (0.0, -1.0)}
+    at = at % count
+    if 4 * at % count == 0:
+        return exact[4 * at // count]
+    return math.cos(2.0 * math.pi * at / count), math.sin(2.0 * math.pi * at / count)
+
+
+def weighted(terms):
+    total = None
+    for weight, array in terms:
+        if weight == 0.0 or array is None:
+            continue
+        if total is None:
+            total = array if weight == 1.0 else -array if weight == -1.0 else array * weight
+        elif weight == 1.0:
+            total = total + array
+        elif weight == -1.0:
+            total = total - array
+        else:
+            total = total + array * weight
+    return total
+
+
+def transform_tables(devices, fast, scale):
+    slow = 2 * devices
+    length = slow * fast
+    at = np.arange(fast)
+    cos, sin = table(2.0 * np.pi / fast * (at[:, None] * at[None, :] % fast))
+    matrix = np.block([[cos, -sin], [sin, cos]]).astype(np.float32)
+    high = matrix.astype(jnp.bfloat16)
+    low = (matrix - high.astype(np.float32)).astype(jnp.bfloat16)
+    rows = np.arange(devices + 1)
+    cos, sin = table(2.0 * np.pi / length * (rows[:, None] * at[None, :] % length))
+    weight = np.where((rows == 0) | (rows == devices), 1.0, 2.0)[:, None] * scale / length
+    turns = np.concatenate([cos, sin, cos * weight, sin * weight]).astype(np.float32)
+    return high, low, turns
+
+
+def product(left, high, low):
+    left_high = left.astype(jnp.bfloat16)
+    left_low = (left - left_high.astype(jnp.float32)).astype(jnp.bfloat16)
+
+    def dot(a, b):
+        return jnp.dot(a, b, preferred_element_type=jnp.float32)
+
+    return dot(left_high, high) + (dot(left_low, high) + dot(left_high, low))
+
+
+def gate_kernel(streams_ref, filter_ref, upstream_ref, out_ref):
+    devices, stacked, fast = out_ref.shape
+    group = stacked // 3
+    query_part = streams_ref[0].astype(jnp.float32)
+    key_part = streams_ref[1].astype(jnp.float32)
+    value_part = streams_ref[2].astype(jnp.float32)
+    upstream = upstream_ref[...].astype(jnp.float32)
+    out_ref[:, :group] = (key_part * value_part).reshape(devices, group, fast)
+    out_ref[:, group : 2 * group] = filter_ref[...].reshape(devices, group, fast)
+    out_ref[:, 2 * group :] = (query_part * upstream).reshape(devices, group, fast)
+
+
+def convolve_kernel(signal_ref, high_ref, low_ref, turns_ref, out_ref):
+    devices, stacked, fast = signal_ref.shape
+    slow, group = 2 * devices, stacked // 3
+    count = devices + 1
+
+    def turn(which, k):
+        return turns_ref[which * count + k : which * count + k + 1, :]
+
+    signal = [signal_ref[a] for a in range(devices)]
+    real, imag = [None] * count, [None] * count
+    for k in range(devices // 2 + 1):
+        sums = [
+            weighted([(circle(slow, a * k)[part], signal[a]) for a in range(parity, devices, 2)])
+            for part in range(2)
+            for parity in range(2)
+        ]
+        cos_even, cos_odd, sin_even, sin_odd = sums
+        real[k] = weighted([(1.0, cos_even), (1.0, cos_odd)])
+        imag[k] = weighted([(-1.0, sin_even), (-1.0, sin_odd)])
+        if 2 * k != devices:
+            real[devices - k] = weighted([(1.0, cos_even), (-1.0, cos_odd)])
+            imag[devices - k] = weighted([(1.0, sin_even), (-1.0, sin_odd)])
+    rows = []
+    for k in range(count):
+        cos, sin = turn(0, k), turn(1, k)
+        if k == 0:
+            turned = (real[k], jnp.zeros_like(real[k]))
+        elif imag[k] is None:
+            turned = (real[k] * cos, -(real[k] * sin))
+        else:
+            turned = (real[k] * cos + imag[k] * sin, imag[k] * cos - real[k] * sin)
+        rows.append(jnp.concatenate(turned, axis=1))
+    high, low = high_ref[...], low_ref[...]
+    spectrum = product(jnp.concatenate(rows, axis=0), high, low)
+    rows = []
+    for k in range(count):
+        base = k * stacked
+        parts = [spectrum[base + i * group : base + (i + 1) * group] for i in range(3)]
+        (gated_real, taps_real, grad_real) = (p[:, :fast] for p in parts)
+        (gated_imag, taps_imag, grad_imag) = (p[:, fast:] for p in parts)
+        rows.append(
+            jnp.concatenate(
+                [
+                    jnp.concatenate(
+                        [
+                            gated_real * taps_real - gated_imag * taps_imag,
+                            -(gated_real * taps_imag + gated_imag * taps_real),
+                        ],
+                        axis=1,
+                    ),
+                    jnp.concatenate(
+                        [
+                            grad_real * taps_real + grad_imag * taps_imag,
+                            grad_real * taps_imag - grad_imag * taps_real,
+                        ],
+                        axis=1,
+                    ),
+                    jnp.concatenate(
+                        [
+                            grad_real * gated_real + grad_imag * gated_imag,
+                            grad_real * gated_imag - grad_imag * gated_real,
+                        ],
+                        axis=1,
+                    ),
+                ],
+                axis=0,
+            )
+        )
+    back = product(jnp.concatenate(rows, axis=0), high, low)
+    real, imag = [], []
+    for k in range(count):
+        cos, sin = turn(2, k), turn(3, k)
+        row = back[k * stacked : (k + 1) * stacked]
+        real.append(row[:, :fast] * cos + row[:, fast:] * sin)
+        imag.append(row[:, fast:] * cos - row[:, :fast] * sin)
+    half = devices // 2
+    for parity in range(2):
+        sign = 1.0 - 2.0 * parity
+        cos_part = [weighted([(1.0, real[k]), (sign, real[devices - k])]) for k in range(half)]
+        sin_part = [weighted([(1.0, imag[k]), (-sign, imag[devices - k])]) for k in range(half)]
+        for a in range(parity, devices, 2):
+            terms = [(circle(slow, a * k)[0], cos_part[k]) for k in range(half)]
+            terms += [(circle(slow, a * k)[1], sin_part[k]) for k in range(1, half)]
+            terms += [(circle(slow, a * half)[0], real[half]), (circle(slow, a * half)[1], imag[half])]
+            out_ref[a] = weighted(terms)
+
+
+def output_kernel(back_ref, streams_ref, upstream_ref, mixed_ref, streams_grad_ref, filter_grad_ref):
+    channels, fast = filter_grad_ref.shape
+    group = back_ref.shape[1] // 3
+    long_conv = back_ref[:, :group].reshape(channels, fast)
+    grad_gated = back_ref[:, group : 2 * group].reshape(channels, fast)
+    filter_grad_ref[...] = back_ref[:, 2 * group :].reshape(channels, fast)
+    mixed_ref[...] = (streams_ref[0].astype(jnp.float32) * long_conv).astype(jnp.bfloat16)
+    streams_grad_ref[0] = (upstream_ref[...].astype(jnp.float32) * long_conv).astype(jnp.bfloat16)
+    streams_grad_ref[1] = (streams_ref[2].astype(jnp.float32) * grad_gated).astype(jnp.bfloat16)
+    streams_grad_ref[2] = (streams_ref[1].astype(jnp.float32) * grad_gated).astype(jnp.bfloat16)
+
+
+def by_channel(streams, filter_raw, grad_output):
+    devices = lax.axis_size("ctx")
+    channels, fast = filter_raw.shape
+    stacked = 3 * (channels // devices)
+    tap_scale = 1.0 / math.sqrt(fast * devices)
+    vmem = pl.BlockSpec(memory_space=pltpu.VMEM)
+    regrouped = jax.ShapeDtypeStruct((devices, stacked, fast), jnp.float32)
+    signals = pl.pallas_call(gate_kernel, out_shape=regrouped, in_specs=[vmem] * 3, out_specs=vmem)(
+        streams, filter_raw, grad_output
+    )
+    signals = lax.all_to_all(signals, "ctx", split_axis=0, concat_axis=0, tiled=True)
+    tables = transform_tables(devices, fast, tap_scale)
+    results = pl.pallas_call(convolve_kernel, out_shape=regrouped, in_specs=[vmem] * 4, out_specs=vmem)(
+        signals, *tables
+    )
+    results = lax.all_to_all(results, "ctx", split_axis=0, concat_axis=0, tiled=True)
+    return pl.pallas_call(
+        output_kernel,
+        out_shape=(
+            jax.ShapeDtypeStruct((channels, fast), jnp.bfloat16),
+            jax.ShapeDtypeStruct((3, channels, fast), jnp.bfloat16),
+            jax.ShapeDtypeStruct((channels, fast), jnp.float32),
+        ),
+        in_specs=[vmem] * 3,
+        out_specs=(vmem,) * 3,
+    )(results, streams, grad_output)
+
+
+def local(streams, filter_raw, grad_output):
+    devices = lax.axis_size("ctx")
+    channels, fast = filter_raw.shape
+    if devices % 2 == 0 and channels % (8 * devices) == 0 and fast % 128 == 0:
+        return by_channel(streams, filter_raw, grad_output)
+    return by_residue(streams, filter_raw, grad_output)
+
+
 def solution(mesh):
     in_specs = (P(None, "tp", "ctx"), P("tp", "ctx"), P("tp", "ctx"))
     out_specs = (P("tp", "ctx"), P(None, "tp", "ctx"), P("tp", "ctx"))

time: 152 us -> 31.9 us (0.21)
  waiting for transfers between devices: 54.2 us -> 0 us
  starting transfers between devices: 47.2 us -> 0 us
  blocking collectives: 0 us -> 25.6 us
  local copies, waits for them, and re-layouts: 24.9 us -> 0 us
  other arithmetic: 12.8 us -> 0 us
  matrix products: 10.4 us -> 0 us
  Pallas kernels: 0 us -> 5.28 us
    all_to_all x12 -> x0, waiting for transfers between devices: 54.2 us -> none  [the longest x2 11.3 us: inverse_signal(): lax.all_to_all(timeline, 'ctx', split_axis=1, concat_axis=3, tiled=True)]
    all_to_all x12 -> x0, starting transfers between devices: 47.2 us -> none  [the longest x2 10.6 us: forward_spectrum(): lax.all_to_all(signal[:, None], 'ctx', split_axis=3, concat_axis=1, tiled...]
    all_to_all x0 -> x2, blocking collectives: none -> 25.6 us  [the longest x1 14.5 us: by_channel(): lax.all_to_all(signals, 'ctx', split_axis=0, concat_axis=0, tiled=True)]
    unnamed x37 -> x0, local copies, waits for them, and re-layouts: 15.3 us -> none
    dot_general x24 -> x0, matrix products: 10.4 us -> none  [the longest x2 1.08 us: forward_spectrum(): jnp.matmul(rows_real, sin_fast, precision=highest)]
    all_to_all x12 -> x0, other arithmetic: 10 us -> none  [the longest x2 1.75 us: inverse_signal(): lax.all_to_all(back_real, 'ctx', split_axis=3, concat_axis=1, tiled=True)]
    pallas_call x0 -> x3, Pallas kernels: none -> 5.28 us  [the longest x1 2.25 us: by_channel(): pl.pallas_call(convolve_kernel, out_shape=regrouped, in_specs=[vmem] * 4,...]
    all_to_all x19 -> x0, local copies, waits for them, and re-layouts: 3.36 us -> none  [the longest x6 1.48 us: inverse_signal(): lax.all_to_all(back_imag, 'ctx', split_axis=3, concat_axis=1, tiled=True)]
  transfers between devices with their start and end apart: 12 -> 0, of which waited for: 11 -> 0; matrix products, arithmetic and copies ran while one was open for 19% -> 0% of each run, Pallas kernels for 0% -> 0%
where the time goes in v1:
time: 31.9 us; the launch traced here: 31.5 us
  blocking collectives  25.6 us (80%)
  Pallas kernels  5.28 us (17%)
  between operations  0.63 us (2%)
    all_to_all x1, blocking collectives, by_channel(): lax.all_to_all(signals, 'ctx', split_axis=0, concat_axis=0, tiled=True)  14.5 us
    all_to_all x1, blocking collectives, by_channel(): lax.all_to_all(results, 'ctx', split_axis=0, concat_axis=0, tiled=True)  11.1 us
    pallas_call x1, Pallas kernels, by_channel(): pl.pallas_call(convolve_kernel, out_shape=regrouped, in_specs=[vmem] * 4,...  2.25 us
    pallas_call x1, Pallas kernels, by_channel(): pl.pallas_call(output_kernel, out_shape=(jax.ShapeDtypeStruct((channels,...  1.57 us
    pallas_call x1, Pallas kernels, by_channel(): pl.pallas_call(gate_kernel, out_shape=regrouped, in_specs=[vmem] * 3, out...  1.46 us

profile of v1, /device:TPU:0, one launch (start us, length us, event | category | flops | bytes accessed | tf_op | source)
XLA Modules:
  0.0 31.5 jit_solution(11319619542239416913)
XLA Ops:
  0.6 1.5 %shard_map.85 = f32[8,24,128]{2,1,0:T(8,128)} custom-call(bf16[3,64,128]{2,1,0:T(8,128)(2,1)} %streams_ref.3, f32[64,128]{1,0:T(8,128)} %filter_ref.1, bf16[64,128]{1,0:T(8,128)(2,1)} %upstream_ref.3), custom_call_target="tpu_custom_call" | custom-call | tf_op jit(solution)/shard_map/pallas_call | solution.py:326
  2.1 14.5 %all_to_all.10.signal_ref = f32[8,24,128]{2,1,0:T(8,128)} all-to-all(f32[8,24,128]{2,1,0:T(8,128)} %shard_map.85), channel_id=1, replica_groups=mesh['ctx'=8,'tp'=4] {'ctx'}, dimensions={0} | all-to-all | bytes 196608 | tf_op jit(solution)/shard_map/all_to_all | solution.py:329
  16.6 2.3 %shard_map.86 = f32[8,24,128]{2,1,0:T(8,128)} custom-call(f32[8,24,128]{2,1,0:T(8,128)} %all_to_all.10.signal_ref, bf16[256,256]{1,0:T(8,128)(2,1)} %constant.6.clone.high_ref, bf16[256,256]{1,0:T(8,128)(2,1)} %constant.7.clone.low_ref, f32[36,128]{1,0:T(8,128)} %constant.8.clone.turns_ref), custom_call_target="tpu_custom_call" | custom-call | tf_op jit(solution)/shard_map/pallas_call | solution.py:331
  18.9 11.1 %all_to_all.11.back_ref = f32[8,24,128]{2,1,0:T(8,128)} all-to-all(f32[8,24,128]{2,1,0:T(8,128)} %shard_map.86), channel_id=1, replica_groups=mesh['ctx'=8,'tp'=4] {'ctx'}, dimensions={0} | all-to-all | bytes 196608 | tf_op jit(solution)/shard_map/all_to_all | solution.py:334
  29.9 1.6 %shard_map.87 = (bf16[64,128]{1,0:T(8,128)(2,1)}, bf16[3,64,128]{2,1,0:T(8,128)(2,1)}, f32[64,128]{1,0:T(8,128)}) custom-call(f32[8,24,128]{2,1,0:T(8,128)} %all_to_all.11.back_ref, bf16[3,64,128]{2,1,0:T(8,128)(2,1)} %streams_ref.3, bf16[64,128]{1,0:T(8,128)(2,1)} %upstream_ref.3), custom_call_target="tpu_custom_call" | custom-call | tf_op jit(solution)/shard_map/pallas_call | solution.py:335

commit v2 on v1

--- a/solution.py
+++ b/solution.py
@@ -205,9 +205,19 @@
     return dot(left_high, high) + (dot(left_low, high) + dot(left_high, low))
 
 
-def gate_kernel(streams_ref, filter_ref, upstream_ref, out_ref):
+def gate_kernel(streams_hbm, filter_hbm, upstream_hbm, out_ref, streams_ref, filter_ref, upstream_ref, arrived):
     devices, stacked, fast = out_ref.shape
     group = stacked // 3
+    loads = [
+        pltpu.make_async_copy(source, target, arrived.at[i])
+        for i, (source, target) in enumerate(
+            [(streams_hbm, streams_ref), (upstream_hbm, upstream_ref), (filter_hbm, filter_ref)]
+        )
+    ]
+    for load in loads:
+        load.start()
+    for load in loads:
+        load.wait()
     query_part = streams_ref[0].astype(jnp.float32)
     key_part = streams_ref[1].astype(jnp.float32)
     value_part = streams_ref[2].astype(jnp.float32)
@@ -322,13 +332,24 @@
     stacked = 3 * (channels // devices)
     tap_scale = 1.0 / math.sqrt(fast * devices)
     vmem = pl.BlockSpec(memory_space=pltpu.VMEM)
+    params = pltpu.CompilerParams(vmem_limit_bytes=8 << 20)
     regrouped = jax.ShapeDtypeStruct((devices, stacked, fast), jnp.float32)
-    signals = pl.pallas_call(gate_kernel, out_shape=regrouped, in_specs=[vmem] * 3, out_specs=vmem)(
-        streams, filter_raw, grad_output
-    )
+    signals = pl.pallas_call(
+        gate_kernel,
+        out_shape=regrouped,
+        in_specs=[pl.BlockSpec(memory_space=pltpu.HBM)] * 3,
+        out_specs=vmem,
+        scratch_shapes=[
+            pltpu.VMEM(streams.shape, streams.dtype),
+            pltpu.VMEM(filter_raw.shape, filter_raw.dtype),
+            pltpu.VMEM(grad_output.shape, grad_output.dtype),
+            pltpu.SemaphoreType.DMA((3,)),
+        ],
+        compiler_params=params,
+    )(*(pltpu.with_memory_space_constraint(x, pltpu.HBM) for x in (streams, filter_raw, grad_output)))
     signals = lax.all_to_all(signals, "ctx", split_axis=0, concat_axis=0, tiled=True)
     tables = transform_tables(devices, fast, tap_scale)
-    results = pl.pallas_call(convolve_kernel, out_shape=regrouped, in_specs=[vmem] * 4, out_specs=vmem)(
+    results = pl.pallas_call(convolve_kernel, out_shape=regrouped, in_specs=[vmem] * 4, out_specs=vmem, compiler_params=params)(
         signals, *tables
     )
     results = lax.all_to_all(results, "ctx", split_axis=0, concat_axis=0, tiled=True)
@@ -341,6 +362,7 @@
         ),
         in_specs=[vmem] * 3,
         out_specs=(vmem,) * 3,
+        compiler_params=params,
     )(results, streams, grad_output)
 
 

time: 31.9 us -> 27.1 us (0.85)
  Pallas kernels: 5.28 us -> 2.12 us
  blocking collectives: 25.6 us -> 24 us
    pallas_call x1, Pallas kernels: 2.25 us -> 0.6 us  [by_channel(): pl.pallas_call(convolve_kernel, out_shape=regrouped, in_specs=[vmem] * 4,...]
    all_to_all x1, blocking collectives: 11.1 us -> 9.64 us  [by_channel(): lax.all_to_all(results, 'ctx', split_axis=0, concat_axis=0, tiled=True)]
    pallas_call x1, Pallas kernels: 1.57 us -> 0.65 us  [by_channel(): pl.pallas_call(output_kernel, out_shape=(jax.ShapeDtypeStruct((channels,...]
    pallas_call x1, Pallas kernels: 1.46 us -> 0.87 us  [by_channel(): pl.pallas_call(gate_kernel, out_shape=regrouped, in_specs=[pl.BlockSpec(m...]
where the time goes in v2:
time: 27.1 us; the launch traced here: 26.8 us
  blocking collectives  24 us (89%)
  Pallas kernels  2.12 us (8%)
  between operations  0.69 us (3%)
    all_to_all x1, blocking collectives, by_channel(): lax.all_to_all(signals, 'ctx', split_axis=0, concat_axis=0, tiled=True)  14.3 us
    all_to_all x1, blocking collectives, by_channel(): lax.all_to_all(results, 'ctx', split_axis=0, concat_axis=0, tiled=True)  9.64 us
    pallas_call x1, Pallas kernels, by_channel(): pl.pallas_call(gate_kernel, out_shape=regrouped, in_specs=[pl.BlockSpec(m...  0.87 us
    pallas_call x1, Pallas kernels, by_channel(): pl.pallas_call(output_kernel, out_shape=(jax.ShapeDtypeStruct((channels,...  0.65 us
    pallas_call x1, Pallas kernels, by_channel(): pl.pallas_call(convolve_kernel, out_shape=regrouped, in_specs=[vmem] * 4,...  0.6 us

profile of v2, /device:TPU:0, one launch (start us, length us, event | category | flops | bytes accessed | tf_op | source)
XLA Modules:
  0.0 26.8 jit_solution(4007343705561903542)
XLA Ops:
  0.6 0.0 copy-start.2
  0.6 0.9 %shard_map.85 = f32[8,24,128]{2,1,0:T(8,128)S(1)} custom-call(bf16[3,64,128]{2,1,0:T(8,128)(2,1)} %streams_ref.1, f32[64,128]{1,0:T(8,128)} %filter_hbm.1, bf16[64,128]{1,0:T(8,128)(2,1)} %upstream_ref.1), custom_call_target="tpu_custom_call" | custom-call | tf_op jit(solution)/shard_map/pallas_call | solution.py:337
  1.5 0.0 copy-start.1
  1.5 0.0 copy-start.4
  1.5 14.3 %all_to_all.10.signal_ref = f32[8,24,128]{2,1,0:T(8,128)S(1)} all-to-all(f32[8,24,128]{2,1,0:T(8,128)S(1)} %shard_map.85), channel_id=1, replica_groups=mesh['ctx'=8,'tp'=4] {'ctx'}, dimensions={0} | all-to-all | bytes 196608 | tf_op jit(solution)/shard_map/all_to_all | solution.py:350
  15.9 0.0 copy-done.2
  15.9 0.0 copy-done.1
  15.9 0.0 copy-done.4
  15.9 0.6 %shard_map.86 = f32[8,24,128]{2,1,0:T(8,128)S(1)} custom-call(f32[8,24,128]{2,1,0:T(8,128)S(1)} %all_to_all.10.signal_ref, bf16[256,256]{1,0:T(8,128)(2,1)S(1)} %copy-done.2, bf16[256,256]{1,0:T(8,128)(2,1)S(1)} %copy-done.1, f32[36,128]{1,0:T(8,128)S(1)} %copy-done.4), custom_call_target="tpu_custom_call" | custom-call | tf_op jit(solution)/shard_map/pallas_call | solution.py:352
  16.5 0.0 copy-start
  16.5 0.0 copy-start.3
  16.5 9.6 %all_to_all.11.back_ref = f32[8,24,128]{2,1,0:T(8,128)S(1)} all-to-all(f32[8,24,128]{2,1,0:T(8,128)S(1)} %shard_map.86), channel_id=1, replica_groups=mesh['ctx'=8,'tp'=4] {'ctx'}, dimensions={0} | all-to-all | bytes 196608 | tf_op jit(solution)/shard_map/all_to_all | solution.py:355
  26.2 0.0 copy-done
  26.2 0.0 copy-done.3
  26.2 0.6 %shard_map.87 = (bf16[64,128]{1,0:T(8,128)(2,1)}, bf16[3,64,128]{2,1,0:T(8,128)(2,1)}, f32[64,128]{1,0:T(8,128)}) custom-call(f32[8,24,128]{2,1,0:T(8,128)S(1)} %all_to_all.11.back_ref, bf16[3,64,128]{2,1,0:T(8,128)(2,1)S(1)} %copy-done, bf16[64,128]{1,0:T(8,128)(2,1)S(1)} %copy-done.3), custom_call_target="tpu_custom_call" | custom-call | tf_op jit(solution)/shard_map/pallas_call | solution.py:356
Async XLA Ops:
  0.6 15.3 %copy-start.2 = (bf16[256,256]{1,0:T(8,128)(2,1)S(1)}, bf16[256,256]{1,0:T(8,128)(2,1)}, u32[]{:S(2)}) copy-start(bf16[256,256]{1,0:T(8,128)(2,1)} %constant.6.clone.high_ref) | copy-start | bytes 393220
  1.5 14.4 %copy-start.1 = (bf16[256,256]{1,0:T(8,128)(2,1)S(1)}, bf16[256,256]{1,0:T(8,128)(2,1)}, u32[]{:S(2)}) copy-start(bf16[256,256]{1,0:T(8,128)(2,1)} %constant.7.clone.low_ref) | copy-start | bytes 393220
  1.5 14.4 %copy-start.4 = (f32[36,128]{1,0:T(8,128)S(1)}, f32[36,128]{1,0:T(8,128)}, u32[]{:S(2)}) copy-start(f32[36,128]{1,0:T(8,128)} %constant.8.clone.turns_ref) | copy-start | bytes 55300
  16.5 9.7 %copy-start = (bf16[3,64,128]{2,1,0:T(8,128)(2,1)S(1)}, bf16[3,64,128]{2,1,0:T(8,128)(2,1)}, u32[]{:S(2)}) copy-start(bf16[3,64,128]{2,1,0:T(8,128)(2,1)} %streams_ref.1) | copy-start | bytes 147460
  16.5 9.7 %copy-start.3 = (bf16[64,128]{1,0:T(8,128)(2,1)S(1)}, bf16[64,128]{1,0:T(8,128)(2,1)}, u32[]{:S(2)}) copy-start(bf16[64,128]{1,0:T(8,128)(2,1)} %upstream_ref.1) | copy-start | bytes 49156

commit v3 on v2

--- a/solution.py
+++ b/solution.py
@@ -180,7 +180,7 @@
     return total
 
 
-def transform_tables(devices, fast, scale):
+def transform_tables(devices, block, fast, scale):
     slow = 2 * devices
     length = slow * fast
     at = np.arange(fast)
@@ -189,10 +189,22 @@
     high = matrix.astype(jnp.bfloat16)
     low = (matrix - high.astype(np.float32)).astype(jnp.bfloat16)
     rows = np.arange(devices + 1)
-    cos, sin = table(2.0 * np.pi / length * (rows[:, None] * at[None, :] % length))
     weight = np.where((rows == 0) | (rows == devices), 1.0, 2.0)[:, None] * scale / length
-    turns = np.concatenate([cos, sin, cos * weight, sin * weight]).astype(np.float32)
-    return high, low, turns
+    turns = [np.concatenate(table(2.0 * np.pi / length * (rows[:, None] * at[None, :] % length)))]
+    for first in range(0, devices, block):
+        cos, sin = table(2.0 * np.pi / length * (rows[:, None] * (first * fast + at[None, :]) % length))
+        turns.append(np.concatenate([cos * weight, sin * weight]))
+    return high, low, np.stack(turns).astype(np.float32)
+
+
+def by_partner(parts, place):
+    parts = list(parts)
+    step = 1
+    while step < len(parts):
+        crossed = (place & step) != 0
+        parts = [jnp.where(crossed, parts[x ^ step], parts[x]) for x in range(len(parts))]
+        step *= 2
+    return parts
 
 
 def product(left, high, low):
@@ -222,18 +234,21 @@
     key_part = streams_ref[1].astype(jnp.float32)
     value_part = streams_ref[2].astype(jnp.float32)
     upstream = upstream_ref[...].astype(jnp.float32)
-    out_ref[:, :group] = (key_part * value_part).reshape(devices, group, fast)
-    out_ref[:, group : 2 * group] = filter_ref[...].reshape(devices, group, fast)
-    out_ref[:, 2 * group :] = (query_part * upstream).reshape(devices, group, fast)
-
-
-def convolve_kernel(signal_ref, high_ref, low_ref, turns_ref, out_ref):
+    block = streams_ref.shape[1] // group
+    for first in range(0, devices, block):
+        out_ref[first : first + block, :group] = (key_part * value_part).reshape(block, group, fast)
+        out_ref[first : first + block, group : 2 * group] = filter_ref[...].reshape(block, group, fast)
+        out_ref[first : first + block, 2 * group :] = (query_part * upstream).reshape(block, group, fast)
+
+
+def convolve_kernel(signal_ref, high_ref, low_ref, turns_ref, *out_refs):
     devices, stacked, fast = signal_ref.shape
-    slow, group = 2 * devices, stacked // 3
+    slow, group, block = 2 * devices, stacked // 3, len(out_refs)
     count = devices + 1
+    position = lax.axis_index("ctx")
 
     def turn(which, k):
-        return turns_ref[which * count + k : which * count + k + 1, :]
+        return turns_ref[which, k : k + 1, :], turns_ref[which, count + k : count + k + 1, :]
 
     signal = [signal_ref[a] for a in range(devices)]
     real, imag = [None] * count, [None] * count
@@ -251,7 +266,7 @@
             imag[devices - k] = weighted([(1.0, sin_even), (-1.0, sin_odd)])
     rows = []
     for k in range(count):
-        cos, sin = turn(0, k), turn(1, k)
+        cos, sin = turn(0, k)
         if k == 0:
             turned = (real[k], jnp.zeros_like(real[k]))
         elif imag[k] is None:
@@ -298,45 +313,50 @@
     back = product(jnp.concatenate(rows, axis=0), high, low)
     real, imag = [], []
     for k in range(count):
-        cos, sin = turn(2, k), turn(3, k)
+        cos, sin = turn(1 + position // block, k)
         row = back[k * stacked : (k + 1) * stacked]
         real.append(row[:, :fast] * cos + row[:, fast:] * sin)
         imag.append(row[:, fast:] * cos - row[:, :fast] * sin)
     half = devices // 2
+    results = [None] * block
     for parity in range(2):
         sign = 1.0 - 2.0 * parity
         cos_part = [weighted([(1.0, real[k]), (sign, real[devices - k])]) for k in range(half)]
         sin_part = [weighted([(1.0, imag[k]), (-sign, imag[devices - k])]) for k in range(half)]
-        for a in range(parity, devices, 2):
+        for a in range(parity, block, 2):
             terms = [(circle(slow, a * k)[0], cos_part[k]) for k in range(half)]
             terms += [(circle(slow, a * k)[1], sin_part[k]) for k in range(1, half)]
             terms += [(circle(slow, a * half)[0], real[half]), (circle(slow, a * half)[1], imag[half])]
-            out_ref[a] = weighted(terms)
-
-
-def output_kernel(back_ref, streams_ref, upstream_ref, mixed_ref, streams_grad_ref, filter_grad_ref):
-    channels, fast = filter_grad_ref.shape
-    group = back_ref.shape[1] // 3
-    long_conv = back_ref[:, :group].reshape(channels, fast)
-    grad_gated = back_ref[:, group : 2 * group].reshape(channels, fast)
-    filter_grad_ref[...] = back_ref[:, 2 * group :].reshape(channels, fast)
+            results[a] = weighted(terms)
+    for out_ref, result in zip(out_refs, by_partner(results, position % block), strict=True):
+        out_ref[...] = result
+
+
+def output_kernel(streams_ref, upstream_ref, *refs):
+    back_refs, (mixed_ref, streams_grad_ref, filter_grad_ref) = refs[:-3], refs[-3:]
+    channels, _ = filter_grad_ref.shape
+    block = len(back_refs)
+    group = channels // block
+    parts = by_partner([ref[...] for ref in back_refs], lax.axis_index("ctx") % block)
+    long_conv = jnp.concatenate([part[:group] for part in parts], axis=0)
+    grad_gated = jnp.concatenate([part[group : 2 * group] for part in parts], axis=0)
+    filter_grad_ref[...] = jnp.concatenate([part[2 * group :] for part in parts], axis=0)
     mixed_ref[...] = (streams_ref[0].astype(jnp.float32) * long_conv).astype(jnp.bfloat16)
     streams_grad_ref[0] = (upstream_ref[...].astype(jnp.float32) * long_conv).astype(jnp.bfloat16)
     streams_grad_ref[1] = (streams_ref[2].astype(jnp.float32) * grad_gated).astype(jnp.bfloat16)
     streams_grad_ref[2] = (streams_ref[1].astype(jnp.float32) * grad_gated).astype(jnp.bfloat16)
 
 
-def by_channel(streams, filter_raw, grad_output):
+def by_channel(streams, filter_raw, grad_output, block):
     devices = lax.axis_size("ctx")
     channels, fast = filter_raw.shape
-    stacked = 3 * (channels // devices)
+    stacked = 3 * (channels // block)
     tap_scale = 1.0 / math.sqrt(fast * devices)
     vmem = pl.BlockSpec(memory_space=pltpu.VMEM)
     params = pltpu.CompilerParams(vmem_limit_bytes=8 << 20)
-    regrouped = jax.ShapeDtypeStruct((devices, stacked, fast), jnp.float32)
     signals = pl.pallas_call(
         gate_kernel,
-        out_shape=regrouped,
+        out_shape=jax.ShapeDtypeStruct((devices, stacked, fast), jnp.float32),
         in_specs=[pl.BlockSpec(memory_space=pltpu.HBM)] * 3,
         out_specs=vmem,
         scratch_shapes=[
@@ -348,11 +368,17 @@
         compiler_params=params,
     )(*(pltpu.with_memory_space_constraint(x, pltpu.HBM) for x in (streams, filter_raw, grad_output)))
     signals = lax.all_to_all(signals, "ctx", split_axis=0, concat_axis=0, tiled=True)
-    tables = transform_tables(devices, fast, tap_scale)
-    results = pl.pallas_call(convolve_kernel, out_shape=regrouped, in_specs=[vmem] * 4, out_specs=vmem, compiler_params=params)(
-        signals, *tables
-    )
-    results = lax.all_to_all(results, "ctx", split_axis=0, concat_axis=0, tiled=True)
+    results = pl.pallas_call(
+        convolve_kernel,
+        out_shape=[jax.ShapeDtypeStruct((stacked, fast), jnp.float32)] * block,
+        in_specs=[vmem] * 4,
+        out_specs=[vmem] * block,
+        compiler_params=params,
+    )(signals, *transform_tables(devices, block, fast, tap_scale))
+    results = [
+        result if x == 0 else lax.ppermute(result, "ctx", [(i, i ^ x) for i in range(devices)])
+        for x, result in enumerate(results)
+    ]
     return pl.pallas_call(
         output_kernel,
         out_shape=(
@@ -360,17 +386,18 @@
             jax.ShapeDtypeStruct((3, channels, fast), jnp.bfloat16),
             jax.ShapeDtypeStruct((channels, fast), jnp.float32),
         ),
-        in_specs=[vmem] * 3,
+        in_specs=[vmem] * (2 + block),
         out_specs=(vmem,) * 3,
         compiler_params=params,
-    )(results, streams, grad_output)
+    )(streams, grad_output, *results)
 
 
 def local(streams, filter_raw, grad_output):
     devices = lax.axis_size("ctx")
     channels, fast = filter_raw.shape
-    if devices % 2 == 0 and channels % (8 * devices) == 0 and fast % 128 == 0:
-        return by_channel(streams, filter_raw, grad_output)
+    block = 4
+    if devices % block == 0 and devices <= 16 and channels % (16 * block) == 0 and fast % 128 == 0:
+        return by_channel(streams, filter_raw, grad_output, block)
     return by_residue(streams, filter_raw, grad_output)
 
 

time: 27.1 us -> 24.7 us (0.911)
  blocking collectives: 24 us -> 15.2 us
  starting transfers between devices: 0 us -> 3.55 us
  waiting for transfers between devices: 0 us -> 2.63 us
  Pallas kernels: 2.12 us -> 2.4 us
    all_to_all x1 -> x0, blocking collectives: 9.64 us -> none  [by_channel(): lax.all_to_all(results, 'ctx', split_axis=0, concat_axis=0, tiled=True)]
    ppermute x0 -> x3, starting transfers between devices: none -> 3.55 us  [by_channel(): lax.ppermute(result, 'ctx', [(i, i ^ x) for i in range(devices)])]
    ppermute x0 -> x3, waiting for transfers between devices: none -> 2.63 us  [by_channel(): lax.ppermute(result, 'ctx', [(i, i ^ x) for i in range(devices)])]
    all_to_all x1, blocking collectives: 14.3 us -> 15.2 us  [by_channel(): lax.all_to_all(signals, 'ctx', split_axis=0, concat_axis=0, tiled=True)]
  transfers between devices with their start and end apart: 0 -> 3, of which waited for: 0 -> 3; matrix products, arithmetic and copies ran while one was open for 0% -> 0% of each run, Pallas kernels for 0% -> 0%
where the time goes in v3:
time: 24.7 us; the launch traced here: 24.5 us
  blocking collectives  15.2 us (62%)
  starting transfers between devices  3.55 us (14%)
  waiting for transfers between devices  2.63 us (11%)
  Pallas kernels  2.4 us (10%)
  between operations  0.69 us (3%)
    all_to_all x1, blocking collectives, by_channel(): lax.all_to_all(signals, 'ctx', split_axis=0, concat_axis=0, tiled=True)  15.2 us
    ppermute x3, starting transfers between devices, by_channel(): lax.ppermute(result, 'ctx', [(i, i ^ x) for i in range(devices)])  3.55 us
    ppermute x3, waiting for transfers between devices, by_channel(): lax.ppermute(result, 'ctx', [(i, i ^ x) for i in range(devices)])  2.63 us
    pallas_call x1, Pallas kernels, by_channel(): pl.pallas_call(convolve_kernel, out_shape=[jax.ShapeDtypeStruct((stacked,...  0.9 us
    pallas_call x1, Pallas kernels, by_channel(): pl.pallas_call(gate_kernel, out_shape=jax.ShapeDtypeStruct((devices, stac...  0.85 us
    pallas_call x1, Pallas kernels, by_channel(): pl.pallas_call(output_kernel, out_shape=(jax.ShapeDtypeStruct((channels,...  0.65 us
  transfers between devices with their start and end apart: 3, of which 3 were waited for; matrix products, arithmetic and copies ran while one was open for 0% of the time, Pallas kernels for 0%

profile of v3, /device:TPU:0, one launch (start us, length us, event | category | flops | bytes accessed | tf_op | source)
XLA Modules:
  0.0 24.5 jit_solution(16734193899433080664)
XLA Ops:
  0.6 0.8 %shard_map.85 = f32[8,48,128]{2,1,0:T(8,128)S(1)} custom-call(bf16[3,64,128]{2,1,0:T(8,128)(2,1)} %streams_ref.1, f32[64,128]{1,0:T(8,128)} %filter_hbm.1, bf16[64,128]{1,0:T(8,128)(2,1)} %upstream_ref.1), custom_call_target="tpu_custom_call" | custom-call | tf_op jit(solution)/shard_map/pallas_call | solution.py:357
  1.5 0.0 copy-start.1
  1.5 0.0 copy-start.2
  1.5 0.0 copy-start.4
  1.5 15.2 %all_to_all.5.signal_ref = f32[8,48,128]{2,1,0:T(8,128)S(1)} all-to-all(f32[8,48,128]{2,1,0:T(8,128)S(1)} %shard_map.85), channel_id=1, replica_groups=mesh['ctx'=8,'tp'=4] {'ctx'}, dimensions={0} | all-to-all | bytes 393216 | tf_op jit(solution)/shard_map/all_to_all | solution.py:370
  16.7 0.0 copy-done.1
  16.7 0.0 copy-done.2
  16.7 0.0 copy-done.4
  16.7 0.0 copy-start
  16.7 0.0 copy-start.3
  16.7 0.9 %shard_map.86 = (f32[48,128]{1,0:T(8,128)S(1)}, f32[48,128]{1,0:T(8,128)S(1)}, f32[48,128]{1,0:T(8,128)S(1)}, f32[48,128]{1,0:T(8,128)S(1)}) custom-call(f32[8,48,128]{2,1,0:T(8,128)S(1)} %all_to_all.5.signal_ref, bf16[256,256]{1,0:T(8,128)(2,1)S(1)} %copy-done.2, bf16[256,256]{1,0:T(8,128)(2,1)S(1)} %copy-done.1, f32[3,18,128]{2,1,0:T(8,128)S(1)} %copy-done.4), custom_call_target="tpu_custom_call" | custom-call | tf_op jit(solution)/shard_map/pallas_call | solution.py:371
  17.6 1.1 %collective-permute-start = (f32[48,128]{1,0:T(8,128)S(1)}, f32[48,128]{1,0:T(8,128)S(1)}, u32[]{:S(2)}, u32[]{:S(2)}) collective-permute-start(f32[48,128]{1,0:T(8,128)S(1)} %get-tuple-element.8), channel_id=1, source_target_pairs={{0,4},{4,0},{8,12},{12,8},{16,20},{20,16},{24,28},{28,24},{1,5},{5... | collective-permute-start | bytes 73736 | tf_op jit(solution)/shard_map/ppermute | solution.py:379
  18.8 0.3 %collective-permute-start.1 = (f32[48,128]{1,0:T(8,128)S(1)}, f32[48,128]{1,0:T(8,128)S(1)}, u32[]{:S(2)}, u32[]{:S(2)}) collective-permute-start(f32[48,128]{1,0:T(8,128)S(1)} %get-tuple-element.9), channel_id=1, source_target_pairs={{0,8},{4,12},{8,0},{12,4},{16,24},{20,28},{24,16},{28,20},{1,9},{5... | collective-permute-start | bytes 73736 | tf_op jit(solution)/shard_map/ppermute | solution.py:379
  19.1 2.1 %collective-permute-start.2 = (f32[48,128]{1,0:T(8,128)S(1)}, f32[48,128]{1,0:T(8,128)S(1)}, u32[]{:S(2)}, u32[]{:S(2)}) collective-permute-start(f32[48,128]{1,0:T(8,128)S(1)} %get-tuple-element.10), channel_id=1, source_target_pairs={{0,12},{4,8},{8,4},{12,0},{16,28},{20,24},{24,20},{28,16},{1,13},{... | collective-permute-start | bytes 73736 | tf_op jit(solution)/shard_map/ppermute | solution.py:379
  21.2 0.3 %collective-permute-done.refs_1_ = f32[48,128]{1,0:T(8,128)S(1)} collective-permute-done((f32[48,128]{1,0:T(8,128)S(1)}, f32[48,128]{1,0:T(8,128)S(1)}, u32[]{:S(2)}, u32[]{:S(2)}) %collective-permute-start) | collective-permute-done | bytes 24608 | tf_op jit(solution)/shard_map/ppermute | solution.py:379
  21.5 1.1 %collective-permute-done.1.refs_2_ = f32[48,128]{1,0:T(8,128)S(1)} collective-permute-done((f32[48,128]{1,0:T(8,128)S(1)}, f32[48,128]{1,0:T(8,128)S(1)}, u32[]{:S(2)}, u32[]{:S(2)}) %collective-permute-start.1) | collective-permute-done | bytes 24608 | tf_op jit(solution)/shard_map/ppermute | solution.py:379
  22.6 1.2 %collective-permute-done.2.refs_3_ = f32[48,128]{1,0:T(8,128)S(1)} collective-permute-done((f32[48,128]{1,0:T(8,128)S(1)}, f32[48,128]{1,0:T(8,128)S(1)}, u32[]{:S(2)}, u32[]{:S(2)}) %collective-permute-start.2) | collective-permute-done | bytes 24608 | tf_op jit(solution)/shard_map/ppermute | solution.py:379
  23.8 0.0 copy-done
  23.8 0.0 copy-done.3
  23.8 0.7 %shard_map.87 = (bf16[64,128]{1,0:T(8,128)(2,1)}, bf16[3,64,128]{2,1,0:T(8,128)(2,1)}, f32[64,128]{1,0:T(8,128)}) custom-call(bf16[3,64,128]{2,1,0:T(8,128)(2,1)S(1)} %copy-done, bf16[64,128]{1,0:T(8,128)(2,1)S(1)} %copy-done.3, f32[48,128]{1,0:T(8,128)S(1)} %get-tuple-element.7.refs_0_, f32[48,128]{1,0:T(8,128)S(1)} %collective-permute-done.refs_1_, ...), custom_call_target="tpu_custom_call" | custom-call | tf_op jit(solution)/shard_map/pallas_call | solution.py:382
Async XLA Ops:
  1.5 15.2 %copy-start.1 = (bf16[256,256]{1,0:T(8,128)(2,1)S(1)}, bf16[256,256]{1,0:T(8,128)(2,1)}, u32[]{:S(2)}) copy-start(bf16[256,256]{1,0:T(8,128)(2,1)} %constant.7.clone.low_ref) | copy-start | bytes 393220
  1.5 15.2 %copy-start.2 = (bf16[256,256]{1,0:T(8,128)(2,1)S(1)}, bf16[256,256]{1,0:T(8,128)(2,1)}, u32[]{:S(2)}) copy-start(bf16[256,256]{1,0:T(8,128)(2,1)} %constant.6.clone.high_ref) | copy-start | bytes 393220
  1.5 15.2 %copy-start.4 = (f32[3,18,128]{2,1,0:T(8,128)S(1)}, f32[3,18,128]{2,1,0:T(8,128)}, u32[]{:S(2)}) copy-start(f32[3,18,128]{2,1,0:T(8,128)} %constant.8.clone.turns_ref) | copy-start | bytes 82948
  16.7 7.1 %copy-start = (bf16[3,64,128]{2,1,0:T(8,128)(2,1)S(1)}, bf16[3,64,128]{2,1,0:T(8,128)(2,1)}, u32[]{:S(2)}) copy-start(bf16[3,64,128]{2,1,0:T(8,128)(2,1)} %streams_ref.1) | copy-start | bytes 147460
  16.7 7.1 %copy-start.3 = (bf16[64,128]{1,0:T(8,128)(2,1)S(1)}, bf16[64,128]{1,0:T(8,128)(2,1)}, u32[]{:S(2)}) copy-start(bf16[64,128]{1,0:T(8,128)(2,1)} %upstream_ref.1) | copy-start | bytes 49156
  17.6 3.9 %collective-permute-start = (f32[48,128]{1,0:T(8,128)S(1)}, f32[48,128]{1,0:T(8,128)S(1)}, u32[]{:S(2)}, u32[]{:S(2)}) collective-permute-start(f32[48,128]{1,0:T(8,128)S(1)} %get-tuple-element.8), channel_id=1, source_target_pairs={{0,4},{4,0},{8,12},{12,8},{16,20},{20,16},{24,28},{28,24},{1,5},{5... | collective-permute-start | bytes 73736 | tf_op jit(solution)/shard_map/ppermute | solution.py:379
  18.8 3.8 %collective-permute-start.1 = (f32[48,128]{1,0:T(8,128)S(1)}, f32[48,128]{1,0:T(8,128)S(1)}, u32[]{:S(2)}, u32[]{:S(2)}) collective-permute-start(f32[48,128]{1,0:T(8,128)S(1)} %get-tuple-element.9), channel_id=1, source_target_pairs={{0,8},{4,12},{8,0},{12,4},{16,24},{20,28},{24,16},{28,20},{1,9},{5... | collective-permute-start | bytes 73736 | tf_op jit(solution)/shard_map/ppermute | solution.py:379
  19.1 4.7 %collective-permute-start.2 = (f32[48,128]{1,0:T(8,128)S(1)}, f32[48,128]{1,0:T(8,128)S(1)}, u32[]{:S(2)}, u32[]{:S(2)}) collective-permute-start(f32[48,128]{1,0:T(8,128)S(1)} %get-tuple-element.10), channel_id=1, source_target_pairs={{0,12},{4,8},{8,4},{12,0},{16,28},{20,24},{24,20},{28,16},{1,13},{... | collective-permute-start | bytes 73736 | tf_op jit(solution)/shard_map/ppermute | solution.py:379

commit v4 on v3

--- a/solution.py
+++ b/solution.py
@@ -214,7 +214,14 @@
     def dot(a, b):
         return jnp.dot(a, b, preferred_element_type=jnp.float32)
 
-    return dot(left_high, high) + (dot(left_low, high) + dot(left_high, low))
+    half = left.shape[0] // 2 // 16 * 16
+    return jnp.concatenate(
+        [
+            dot(left_high[part], high) + (dot(left_low[part], high) + dot(left_high[part], low))
+            for part in (slice(0, half), slice(half, left.shape[0]))
+        ],
+        axis=0,
+    )
 
 
 def gate_kernel(streams_hbm, filter_hbm, upstream_hbm, out_ref, streams_ref, filter_ref, upstream_ref, arrived):
@@ -337,7 +344,7 @@
     channels, _ = filter_grad_ref.shape
     block = len(back_refs)
     group = channels // block
-    parts = by_partner([ref[...] for ref in back_refs], lax.axis_index("ctx") % block)
+    parts = by_partner([back_refs[k][...] for k in [0, 2, 3, 1]], lax.axis_index("ctx") % block)
     long_conv = jnp.concatenate([part[:group] for part in parts], axis=0)
     grad_gated = jnp.concatenate([part[group : 2 * group] for part in parts], axis=0)
     filter_grad_ref[...] = jnp.concatenate([part[2 * group :] for part in parts], axis=0)
@@ -375,10 +382,8 @@
         out_specs=[vmem] * block,
         compiler_params=params,
     )(signals, *transform_tables(devices, block, fast, tap_scale))
-    results = [
-        result if x == 0 else lax.ppermute(result, "ctx", [(i, i ^ x) for i in range(devices)])
-        for x, result in enumerate(results)
-    ]
+    order = (3, 1, 2)
+    results = list(results[:1]) + [lax.ppermute(results[x], "ctx", [(i, i ^ x) for i in range(devices)]) for x in order]
     return pl.pallas_call(
         output_kernel,
         out_shape=(

time: 24.7 us -> 23.9 us (0.968)
  waiting for transfers between devices: 2.63 us -> 2.08 us
    ppermute x3, waiting for transfers between devices: 2.63 us -> 2.08 us  [by_channel(): lax.ppermute(results[x], 'ctx', [(i, i ^ x) for i in range(devices)])]
where the time goes in v4:
time: 23.9 us; the launch traced here: 23.7 us
  blocking collectives  15.2 us (64%)
  starting transfers between devices  3.55 us (15%)
  Pallas kernels  2.2 us (9%)
  waiting for transfers between devices  2.08 us (9%)
  between operations  0.69 us (3%)
    all_to_all x1, blocking collectives, by_channel(): lax.all_to_all(signals, 'ctx', split_axis=0, concat_axis=0, tiled=True)  15.2 us
    ppermute x3, starting transfers between devices, by_channel(): lax.ppermute(results[x], 'ctx', [(i, i ^ x) for i in range(devices)])  3.55 us
    ppermute x3, waiting for transfers between devices, by_channel(): lax.ppermute(results[x], 'ctx', [(i, i ^ x) for i in range(devices)])  2.08 us
    pallas_call x1, Pallas kernels, by_channel(): pl.pallas_call(gate_kernel, out_shape=jax.ShapeDtypeStruct((devices, stac...  0.85 us
    pallas_call x1, Pallas kernels, by_channel(): pl.pallas_call(convolve_kernel, out_shape=[jax.ShapeDtypeStruct((stacked,...  0.7 us
    pallas_call x1, Pallas kernels, by_channel(): pl.pallas_call(output_kernel, out_shape=(jax.ShapeDtypeStruct((channels,...  0.65 us
  transfers between devices with their start and end apart: 3, of which 3 were waited for; matrix products, arithmetic and copies ran while one was open for 0% of the time, Pallas kernels for 0%

profile of v4, /device:TPU:0, one launch (start us, length us, event | category | flops | bytes accessed | tf_op | source)
XLA Modules:
  0.0 23.7 jit_solution(15043254888950699995)
XLA Ops:
  0.6 0.8 %shard_map.85 = f32[8,48,128]{2,1,0:T(8,128)S(1)} custom-call(bf16[3,64,128]{2,1,0:T(8,128)(2,1)} %streams_ref.1, f32[64,128]{1,0:T(8,128)} %filter_hbm.1, bf16[64,128]{1,0:T(8,128)(2,1)} %upstream_ref.1), custom_call_target="tpu_custom_call" | custom-call | tf_op jit(solution)/shard_map/pallas_call | solution.py:364
  1.5 0.0 copy-start.1
  1.5 0.0 copy-start.2
  1.5 0.0 copy-start.4
  1.5 15.2 %all_to_all.5.signal_ref = f32[8,48,128]{2,1,0:T(8,128)S(1)} all-to-all(f32[8,48,128]{2,1,0:T(8,128)S(1)} %shard_map.85), channel_id=1, replica_groups=mesh['ctx'=8,'tp'=4] {'ctx'}, dimensions={0} | all-to-all | bytes 393216 | tf_op jit(solution)/shard_map/all_to_all | solution.py:377
  16.7 0.0 copy-done.1
  16.7 0.0 copy-done.2
  16.7 0.0 copy-done.4
  16.7 0.0 copy-start
  16.7 0.0 copy-start.3
  16.7 0.7 %shard_map.86 = (f32[48,128]{1,0:T(8,128)S(1)}, f32[48,128]{1,0:T(8,128)S(1)}, f32[48,128]{1,0:T(8,128)S(1)}, f32[48,128]{1,0:T(8,128)S(1)}) custom-call(f32[8,48,128]{2,1,0:T(8,128)S(1)} %all_to_all.5.signal_ref, bf16[256,256]{1,0:T(8,128)(2,1)S(1)} %copy-done.2, bf16[256,256]{1,0:T(8,128)(2,1)S(1)} %copy-done.1, f32[3,18,128]{2,1,0:T(8,128)S(1)} %copy-done.4), custom_call_target="tpu_custom_call" | custom-call | tf_op jit(solution)/shard_map/pallas_call | solution.py:378
  17.4 0.9 %collective-permute-start = (f32[48,128]{1,0:T(8,128)S(1)}, f32[48,128]{1,0:T(8,128)S(1)}, u32[]{:S(2)}, u32[]{:S(2)}) collective-permute-start(f32[48,128]{1,0:T(8,128)S(1)} %get-tuple-element.8), channel_id=1, source_target_pairs={{0,12},{4,8},{8,4},{12,0},{16,28},{20,24},{24,20},{28,16},{1,13},{... | collective-permute-start | bytes 73736 | tf_op jit(solution)/shard_map/ppermute | solution.py:386
  18.3 0.9 %collective-permute-start.1 = (f32[48,128]{1,0:T(8,128)S(1)}, f32[48,128]{1,0:T(8,128)S(1)}, u32[]{:S(2)}, u32[]{:S(2)}) collective-permute-start(f32[48,128]{1,0:T(8,128)S(1)} %get-tuple-element.9), channel_id=1, source_target_pairs={{0,4},{4,0},{8,12},{12,8},{16,20},{20,16},{24,28},{28,24},{1,5},{5... | collective-permute-start | bytes 73736 | tf_op jit(solution)/shard_map/ppermute | solution.py:386
  19.2 1.7 %collective-permute-start.2 = (f32[48,128]{1,0:T(8,128)S(1)}, f32[48,128]{1,0:T(8,128)S(1)}, u32[]{:S(2)}, u32[]{:S(2)}) collective-permute-start(f32[48,128]{1,0:T(8,128)S(1)} %get-tuple-element.10), channel_id=1, source_target_pairs={{0,8},{4,12},{8,0},{12,4},{16,24},{20,28},{24,16},{28,20},{1,9},{5... | collective-permute-start | bytes 73736 | tf_op jit(solution)/shard_map/ppermute | solution.py:386
  21.0 1.3 %collective-permute-done.refs_1_ = f32[48,128]{1,0:T(8,128)S(1)} collective-permute-done((f32[48,128]{1,0:T(8,128)S(1)}, f32[48,128]{1,0:T(8,128)S(1)}, u32[]{:S(2)}, u32[]{:S(2)}) %collective-permute-start) | collective-permute-done | bytes 24608 | tf_op jit(solution)/shard_map/ppermute | solution.py:386
  22.3 0.1 collective-permute-done.1.refs_2_
  22.4 0.7 %collective-permute-done.2.refs_3_ = f32[48,128]{1,0:T(8,128)S(1)} collective-permute-done((f32[48,128]{1,0:T(8,128)S(1)}, f32[48,128]{1,0:T(8,128)S(1)}, u32[]{:S(2)}, u32[]{:S(2)}) %collective-permute-start.2) | collective-permute-done | bytes 24608 | tf_op jit(solution)/shard_map/ppermute | solution.py:386
  23.1 0.0 copy-done
  23.1 0.0 copy-done.3
  23.1 0.7 %shard_map.87 = (bf16[64,128]{1,0:T(8,128)(2,1)}, bf16[3,64,128]{2,1,0:T(8,128)(2,1)}, f32[64,128]{1,0:T(8,128)}) custom-call(bf16[3,64,128]{2,1,0:T(8,128)(2,1)S(1)} %copy-done, bf16[64,128]{1,0:T(8,128)(2,1)S(1)} %copy-done.3, f32[48,128]{1,0:T(8,128)S(1)} %get-tuple-element.7.refs_0_, f32[48,128]{1,0:T(8,128)S(1)} %collective-permute-done.refs_1_, ...), custom_call_target="tpu_custom_call" | custom-call | tf_op jit(solution)/shard_map/pallas_call | solution.py:387
Async XLA Ops:
  1.5 15.2 %copy-start.1 = (bf16[256,256]{1,0:T(8,128)(2,1)S(1)}, bf16[256,256]{1,0:T(8,128)(2,1)}, u32[]{:S(2)}) copy-start(bf16[256,256]{1,0:T(8,128)(2,1)} %constant.7.clone.low_ref) | copy-start | bytes 393220
  1.5 15.2 %copy-start.2 = (bf16[256,256]{1,0:T(8,128)(2,1)S(1)}, bf16[256,256]{1,0:T(8,128)(2,1)}, u32[]{:S(2)}) copy-start(bf16[256,256]{1,0:T(8,128)(2,1)} %constant.6.clone.high_ref) | copy-start | bytes 393220
  1.5 15.2 %copy-start.4 = (f32[3,18,128]{2,1,0:T(8,128)S(1)}, f32[3,18,128]{2,1,0:T(8,128)}, u32[]{:S(2)}) copy-start(f32[3,18,128]{2,1,0:T(8,128)} %constant.8.clone.turns_ref) | copy-start | bytes 82948
  16.7 6.4 %copy-start = (bf16[3,64,128]{2,1,0:T(8,128)(2,1)S(1)}, bf16[3,64,128]{2,1,0:T(8,128)(2,1)}, u32[]{:S(2)}) copy-start(bf16[3,64,128]{2,1,0:T(8,128)(2,1)} %streams_ref.1) | copy-start | bytes 147460
  16.7 6.4 %copy-start.3 = (bf16[64,128]{1,0:T(8,128)(2,1)S(1)}, bf16[64,128]{1,0:T(8,128)(2,1)}, u32[]{:S(2)}) copy-start(bf16[64,128]{1,0:T(8,128)(2,1)} %upstream_ref.1) | copy-start | bytes 49156
  17.4 4.9 %collective-permute-start = (f32[48,128]{1,0:T(8,128)S(1)}, f32[48,128]{1,0:T(8,128)S(1)}, u32[]{:S(2)}, u32[]{:S(2)}) collective-permute-start(f32[48,128]{1,0:T(8,128)S(1)} %get-tuple-element.8), channel_id=1, source_target_pairs={{0,12},{4,8},{8,4},{12,0},{16,28},{20,24},{24,20},{28,16},{1,13},{... | collective-permute-start | bytes 73736 | tf_op jit(solution)/shard_map/ppermute | solution.py:386
  18.3 4.1 %collective-permute-start.1 = (f32[48,128]{1,0:T(8,128)S(1)}, f32[48,128]{1,0:T(8,128)S(1)}, u32[]{:S(2)}, u32[]{:S(2)}) collective-permute-start(f32[48,128]{1,0:T(8,128)S(1)} %get-tuple-element.9), channel_id=1, source_target_pairs={{0,4},{4,0},{8,12},{12,8},{16,20},{20,16},{24,28},{28,24},{1,5},{5... | collective-permute-start | bytes 73736 | tf_op jit(solution)/shard_map/ppermute | solution.py:386
  19.2 3.8 %collective-permute-start.2 = (f32[48,128]{1,0:T(8,128)S(1)}, f32[48,128]{1,0:T(8,128)S(1)}, u32[]{:S(2)}, u32[]{:S(2)}) collective-permute-start(f32[48,128]{1,0:T(8,128)S(1)} %get-tuple-element.10), channel_id=1, source_target_pairs={{0,8},{4,12},{8,0},{12,4},{16,24},{20,28},{24,16},{28,20},{1,9},{5... | collective-permute-start | bytes 73736 | tf_op jit(solution)/shard_map/ppermute | solution.py:386

commit v5 on v4

--- a/solution.py
+++ b/solution.py
@@ -224,6 +224,10 @@
     )
 
 
+def exchange_order(devices):
+    return [5, 1, 6, 0, 2, 4, 3, 7] if devices == 8 else list(range(devices))
+
+
 def gate_kernel(streams_hbm, filter_hbm, upstream_hbm, out_ref, streams_ref, filter_ref, upstream_ref, arrived):
     devices, stacked, fast = out_ref.shape
     group = stacked // 3
@@ -237,15 +241,14 @@
         load.start()
     for load in loads:
         load.wait()
-    query_part = streams_ref[0].astype(jnp.float32)
-    key_part = streams_ref[1].astype(jnp.float32)
-    value_part = streams_ref[2].astype(jnp.float32)
-    upstream = upstream_ref[...].astype(jnp.float32)
+    gated_input = streams_ref[1].astype(jnp.float32) * streams_ref[2].astype(jnp.float32)
+    grad_conv = streams_ref[0].astype(jnp.float32) * upstream_ref[...].astype(jnp.float32)
     block = streams_ref.shape[1] // group
-    for first in range(0, devices, block):
-        out_ref[first : first + block, :group] = (key_part * value_part).reshape(block, group, fast)
-        out_ref[first : first + block, group : 2 * group] = filter_ref[...].reshape(block, group, fast)
-        out_ref[first : first + block, 2 * group :] = (query_part * upstream).reshape(block, group, fast)
+    for chunk, device in enumerate(exchange_order(devices)):
+        share = slice(device % block * group, (device % block + 1) * group)
+        out_ref[chunk, :group] = gated_input[share]
+        out_ref[chunk, group : 2 * group] = filter_ref[share]
+        out_ref[chunk, 2 * group :] = grad_conv[share]
 
 
 def convolve_kernel(signal_ref, high_ref, low_ref, turns_ref, *out_refs):
@@ -257,7 +260,8 @@
     def turn(which, k):
         return turns_ref[which, k : k + 1, :], turns_ref[which, count + k : count + k + 1, :]
 
-    signal = [signal_ref[a] for a in range(devices)]
+    order = exchange_order(devices)
+    signal = [signal_ref[order.index(a)] for a in range(devices)]
     real, imag = [None] * count, [None] * count
     for k in range(devices // 2 + 1):
         sums = [
@@ -374,7 +378,9 @@
         ],
         compiler_params=params,
     )(*(pltpu.with_memory_space_constraint(x, pltpu.HBM) for x in (streams, filter_raw, grad_output)))
-    signals = lax.all_to_all(signals, "ctx", split_axis=0, concat_axis=0, tiled=True)
+    signals = lax.all_to_all(
+        signals, "ctx", split_axis=0, concat_axis=0, axis_index_groups=[exchange_order(devices)], tiled=True
+    )
     results = pl.pallas_call(
         convolve_kernel,
         out_shape=[jax.ShapeDtypeStruct((stacked, fast), jnp.float32)] * block,

time: 23.9 us -> 21.5 us (0.90)
  blocking collectives: 15.2 us -> 12.8 us
    all_to_all x1, blocking collectives: 15.2 us -> 12.8 us  [by_channel(): lax.all_to_all(signals, 'ctx', split_axis=0, concat_axis=0, axis_index_gr...]
where the time goes in v5:
time: 21.5 us; the launch traced here: 21.3 us
  blocking collectives  12.8 us (60%)
  starting transfers between devices  3.55 us (17%)
  Pallas kernels  2.2 us (10%)
  waiting for transfers between devices  2.1 us (10%)
  between operations  0.69 us (3%)
    all_to_all x1, blocking collectives, by_channel(): lax.all_to_all(signals, 'ctx', split_axis=0, concat_axis=0, axis_index_gr...  12.8 us
    ppermute x3, starting transfers between devices, by_channel(): lax.ppermute(results[x], 'ctx', [(i, i ^ x) for i in range(devices)])  3.55 us
    ppermute x3, waiting for transfers between devices, by_channel(): lax.ppermute(results[x], 'ctx', [(i, i ^ x) for i in range(devices)])  2.1 us
    pallas_call x1, Pallas kernels, by_channel(): pl.pallas_call(gate_kernel, out_shape=jax.ShapeDtypeStruct((devices, stac...  0.84 us
    pallas_call x1, Pallas kernels, by_channel(): pl.pallas_call(convolve_kernel, out_shape=[jax.ShapeDtypeStruct((stacked,...  0.7 us
    pallas_call x1, Pallas kernels, by_channel(): pl.pallas_call(output_kernel, out_shape=(jax.ShapeDtypeStruct((channels,...  0.65 us
  transfers between devices with their start and end apart: 3, of which 3 were waited for; matrix products, arithmetic and copies ran while one was open for 0% of the time, Pallas kernels for 0%

profile of v5, /device:TPU:0, one launch (start us, length us, event | category | flops | bytes accessed | tf_op | source)
XLA Modules:
  0.0 21.3 jit_solution(17379375327599678971)
XLA Ops:
  0.6 0.8 %shard_map.85 = f32[8,48,128]{2,1,0:T(8,128)S(1)} custom-call(bf16[3,64,128]{2,1,0:T(8,128)(2,1)} %streams_ref.1, f32[64,128]{1,0:T(8,128)} %filter_hbm.1, bf16[64,128]{1,0:T(8,128)(2,1)} %upstream_ref.1), custom_call_target="tpu_custom_call" | custom-call | tf_op jit(solution)/shard_map/pallas_call | solution.py:368
  1.5 0.0 copy-start.1
  1.5 0.0 copy-start.2
  1.5 0.0 copy-start.4
  1.5 12.8 %all_to_all.5.signal_ref = f32[8,48,128]{2,1,0:T(8,128)S(1)} all-to-all(f32[8,48,128]{2,1,0:T(8,128)S(1)} %shard_map.85), channel_id=1, replica_groups={{20,4,24,0,8,16,12,28},{21,5,25,1,9,17,13,29},{22,6,26,2,10,18,14,30},{..., dimensions={0} | all-to-all | bytes 393216 | tf_op jit(solution)/shard_map/all_to_all | solution.py:381
  14.3 0.0 copy-done.1
  14.3 0.0 copy-done.2
  14.3 0.0 copy-done.4
  14.3 0.0 copy-start
  14.3 0.0 copy-start.3
  14.3 0.7 %shard_map.86 = (f32[48,128]{1,0:T(8,128)S(1)}, f32[48,128]{1,0:T(8,128)S(1)}, f32[48,128]{1,0:T(8,128)S(1)}, f32[48,128]{1,0:T(8,128)S(1)}) custom-call(f32[8,48,128]{2,1,0:T(8,128)S(1)} %all_to_all.5.signal_ref, bf16[256,256]{1,0:T(8,128)(2,1)S(1)} %copy-done.2, bf16[256,256]{1,0:T(8,128)(2,1)S(1)} %copy-done.1, f32[3,18,128]{2,1,0:T(8,128)S(1)} %copy-done.4), custom_call_target="tpu_custom_call" | custom-call | tf_op jit(solution)/shard_map/pallas_call | solution.py:384
  15.0 1.6 %collective-permute-start = (f32[48,128]{1,0:T(8,128)S(1)}, f32[48,128]{1,0:T(8,128)S(1)}, u32[]{:S(2)}, u32[]{:S(2)}) collective-permute-start(f32[48,128]{1,0:T(8,128)S(1)} %get-tuple-element.8), channel_id=1, source_target_pairs={{0,12},{4,8},{8,4},{12,0},{16,28},{20,24},{24,20},{28,16},{1,13},{... | collective-permute-start | bytes 73736 | tf_op jit(solution)/shard_map/ppermute | solution.py:392
  16.6 0.2 collective-permute-start.1
  16.8 1.7 %collective-permute-start.2 = (f32[48,128]{1,0:T(8,128)S(1)}, f32[48,128]{1,0:T(8,128)S(1)}, u32[]{:S(2)}, u32[]{:S(2)}) collective-permute-start(f32[48,128]{1,0:T(8,128)S(1)} %get-tuple-element.10), channel_id=1, source_target_pairs={{0,8},{4,12},{8,0},{12,4},{16,24},{20,28},{24,16},{28,20},{1,9},{5... | collective-permute-start | bytes 73736 | tf_op jit(solution)/shard_map/ppermute | solution.py:392
  18.6 1.2 %collective-permute-done.refs_1_ = f32[48,128]{1,0:T(8,128)S(1)} collective-permute-done((f32[48,128]{1,0:T(8,128)S(1)}, f32[48,128]{1,0:T(8,128)S(1)}, u32[]{:S(2)}, u32[]{:S(2)}) %collective-permute-start) | collective-permute-done | bytes 24608 | tf_op jit(solution)/shard_map/ppermute | solution.py:392
  19.8 0.7 %collective-permute-done.1.refs_2_ = f32[48,128]{1,0:T(8,128)S(1)} collective-permute-done((f32[48,128]{1,0:T(8,128)S(1)}, f32[48,128]{1,0:T(8,128)S(1)}, u32[]{:S(2)}, u32[]{:S(2)}) %collective-permute-start.1) | collective-permute-done | bytes 24608 | tf_op jit(solution)/shard_map/ppermute | solution.py:392
  20.5 0.2 collective-permute-done.2.refs_3_
  20.7 0.0 copy-done
  20.7 0.0 copy-done.3
  20.7 0.7 %shard_map.87 = (bf16[64,128]{1,0:T(8,128)(2,1)}, bf16[3,64,128]{2,1,0:T(8,128)(2,1)}, f32[64,128]{1,0:T(8,128)}) custom-call(bf16[3,64,128]{2,1,0:T(8,128)(2,1)S(1)} %copy-done, bf16[64,128]{1,0:T(8,128)(2,1)S(1)} %copy-done.3, f32[48,128]{1,0:T(8,128)S(1)} %get-tuple-element.7.refs_0_, f32[48,128]{1,0:T(8,128)S(1)} %collective-permute-done.refs_1_, ...), custom_call_target="tpu_custom_call" | custom-call | tf_op jit(solution)/shard_map/pallas_call | solution.py:393
Async XLA Ops:
  1.5 12.8 %copy-start.1 = (bf16[256,256]{1,0:T(8,128)(2,1)S(1)}, bf16[256,256]{1,0:T(8,128)(2,1)}, u32[]{:S(2)}) copy-start(bf16[256,256]{1,0:T(8,128)(2,1)} %constant.7.clone.low_ref) | copy-start | bytes 393220
  1.5 12.8 %copy-start.2 = (bf16[256,256]{1,0:T(8,128)(2,1)S(1)}, bf16[256,256]{1,0:T(8,128)(2,1)}, u32[]{:S(2)}) copy-start(bf16[256,256]{1,0:T(8,128)(2,1)} %constant.6.clone.high_ref) | copy-start | bytes 393220
  1.5 12.8 %copy-start.4 = (f32[3,18,128]{2,1,0:T(8,128)S(1)}, f32[3,18,128]{2,1,0:T(8,128)}, u32[]{:S(2)}) copy-start(f32[3,18,128]{2,1,0:T(8,128)} %constant.8.clone.turns_ref) | copy-start | bytes 82948
  14.3 6.4 %copy-start = (bf16[3,64,128]{2,1,0:T(8,128)(2,1)S(1)}, bf16[3,64,128]{2,1,0:T(8,128)(2,1)}, u32[]{:S(2)}) copy-start(bf16[3,64,128]{2,1,0:T(8,128)(2,1)} %streams_ref.1) | copy-start | bytes 147460
  14.3 6.4 %copy-start.3 = (bf16[64,128]{1,0:T(8,128)(2,1)S(1)}, bf16[64,128]{1,0:T(8,128)(2,1)}, u32[]{:S(2)}) copy-start(bf16[64,128]{1,0:T(8,128)(2,1)} %upstream_ref.1) | copy-start | bytes 49156
  15.0 4.8 %collective-permute-start = (f32[48,128]{1,0:T(8,128)S(1)}, f32[48,128]{1,0:T(8,128)S(1)}, u32[]{:S(2)}, u32[]{:S(2)}) collective-permute-start(f32[48,128]{1,0:T(8,128)S(1)} %get-tuple-element.8), channel_id=1, source_target_pairs={{0,12},{4,8},{8,4},{12,0},{16,28},{20,24},{24,20},{28,16},{1,13},{... | collective-permute-start | bytes 73736 | tf_op jit(solution)/shard_map/ppermute | solution.py:392
  16.6 3.8 %collective-permute-start.1 = (f32[48,128]{1,0:T(8,128)S(1)}, f32[48,128]{1,0:T(8,128)S(1)}, u32[]{:S(2)}, u32[]{:S(2)}) collective-permute-start(f32[48,128]{1,0:T(8,128)S(1)} %get-tuple-element.9), channel_id=1, source_target_pairs={{0,4},{4,0},{8,12},{12,8},{16,20},{20,16},{24,28},{28,24},{1,5},{5... | collective-permute-start | bytes 73736 | tf_op jit(solution)/shard_map/ppermute | solution.py:392
  16.8 3.8 %collective-permute-start.2 = (f32[48,128]{1,0:T(8,128)S(1)}, f32[48,128]{1,0:T(8,128)S(1)}, u32[]{:S(2)}, u32[]{:S(2)}) collective-permute-start(f32[48,128]{1,0:T(8,128)S(1)} %get-tuple-element.10), channel_id=1, source_target_pairs={{0,8},{4,12},{8,0},{12,4},{16,24},{20,28},{24,16},{28,20},{1,9},{5... | collective-permute-start | bytes 73736 | tf_op jit(solution)/shard_map/ppermute | solution.py:392

commit v6 on v5

--- a/solution.py
+++ b/solution.py
@@ -180,21 +180,19 @@
     return total
 
 
-def transform_tables(devices, block, fast, scale):
-    slow = 2 * devices
+def transform_tables(block, fast, scale):
+    slow = 2 * block
     length = slow * fast
     at = np.arange(fast)
     cos, sin = table(2.0 * np.pi / fast * (at[:, None] * at[None, :] % fast))
     matrix = np.block([[cos, -sin], [sin, cos]]).astype(np.float32)
     high = matrix.astype(jnp.bfloat16)
     low = (matrix - high.astype(np.float32)).astype(jnp.bfloat16)
-    rows = np.arange(devices + 1)
-    weight = np.where((rows == 0) | (rows == devices), 1.0, 2.0)[:, None] * scale / length
-    turns = [np.concatenate(table(2.0 * np.pi / length * (rows[:, None] * at[None, :] % length)))]
-    for first in range(0, devices, block):
-        cos, sin = table(2.0 * np.pi / length * (rows[:, None] * (first * fast + at[None, :]) % length))
-        turns.append(np.concatenate([cos * weight, sin * weight]))
-    return high, low, np.stack(turns).astype(np.float32)
+    rows = np.arange(block + 1)
+    cos, sin = table(2.0 * np.pi / length * (rows[:, None] * at[None, :] % length))
+    weight = np.where((rows == 0) | (rows == block), 1.0, 2.0)[:, None] * scale / length
+    turns = np.stack([np.concatenate([cos, sin]), np.concatenate([cos * weight, sin * weight])])
+    return high, low, turns.astype(np.float32)
 
 
 def by_partner(parts, place):
@@ -251,94 +249,98 @@
         out_ref[chunk, 2 * group :] = grad_conv[share]
 
 
-def convolve_kernel(signal_ref, high_ref, low_ref, turns_ref, *out_refs):
-    devices, stacked, fast = signal_ref.shape
-    slow, group, block = 2 * devices, stacked // 3, len(out_refs)
-    count = devices + 1
-    position = lax.axis_index("ctx")
-
-    def turn(which, k):
-        return turns_ref[which, k : k + 1, :], turns_ref[which, count + k : count + k + 1, :]
-
-    order = exchange_order(devices)
-    signal = [signal_ref[order.index(a)] for a in range(devices)]
-    real, imag = [None] * count, [None] * count
-    for k in range(devices // 2 + 1):
+def slow_transform(signal, slow):
+    block = slow // 2
+    real, imag = [None] * (block + 1), [None] * (block + 1)
+    for k in range(block // 2 + 1):
         sums = [
-            weighted([(circle(slow, a * k)[part], signal[a]) for a in range(parity, devices, 2)])
+            weighted([(circle(slow, a * k)[part], signal[a]) for a in range(parity, block, 2)])
             for part in range(2)
             for parity in range(2)
         ]
         cos_even, cos_odd, sin_even, sin_odd = sums
         real[k] = weighted([(1.0, cos_even), (1.0, cos_odd)])
         imag[k] = weighted([(-1.0, sin_even), (-1.0, sin_odd)])
-        if 2 * k != devices:
-            real[devices - k] = weighted([(1.0, cos_even), (-1.0, cos_odd)])
-            imag[devices - k] = weighted([(1.0, sin_even), (-1.0, sin_odd)])
-    rows = []
-    for k in range(count):
-        cos, sin = turn(0, k)
-        if k == 0:
-            turned = (real[k], jnp.zeros_like(real[k]))
-        elif imag[k] is None:
-            turned = (real[k] * cos, -(real[k] * sin))
-        else:
-            turned = (real[k] * cos + imag[k] * sin, imag[k] * cos - real[k] * sin)
-        rows.append(jnp.concatenate(turned, axis=1))
-    high, low = high_ref[...], low_ref[...]
-    spectrum = product(jnp.concatenate(rows, axis=0), high, low)
-    rows = []
-    for k in range(count):
-        base = k * stacked
-        parts = [spectrum[base + i * group : base + (i + 1) * group] for i in range(3)]
-        (gated_real, taps_real, grad_real) = (p[:, :fast] for p in parts)
-        (gated_imag, taps_imag, grad_imag) = (p[:, fast:] for p in parts)
-        rows.append(
-            jnp.concatenate(
-                [
-                    jnp.concatenate(
-                        [
-                            gated_real * taps_real - gated_imag * taps_imag,
-                            -(gated_real * taps_imag + gated_imag * taps_real),
-                        ],
-                        axis=1,
-                    ),
-                    jnp.concatenate(
-                        [
-                            grad_real * taps_real + grad_imag * taps_imag,
-                            grad_real * taps_imag - grad_imag * taps_real,
-                        ],
-                        axis=1,
-                    ),
-                    jnp.concatenate(
-                        [
-                            grad_real * gated_real + grad_imag * gated_imag,
-                            grad_real * gated_imag - grad_imag * gated_real,
-                        ],
-                        axis=1,
-                    ),
-                ],
-                axis=0,
-            )
-        )
-    back = product(jnp.concatenate(rows, axis=0), high, low)
-    real, imag = [], []
-    for k in range(count):
-        cos, sin = turn(1 + position // block, k)
-        row = back[k * stacked : (k + 1) * stacked]
-        real.append(row[:, :fast] * cos + row[:, fast:] * sin)
-        imag.append(row[:, fast:] * cos - row[:, :fast] * sin)
-    half = devices // 2
+        if 2 * k != block:
+            real[block - k] = weighted([(1.0, cos_even), (-1.0, cos_odd)])
+            imag[block - k] = weighted([(1.0, sin_even), (-1.0, sin_odd)])
+    return real, imag
+
+
+def slow_inverse(real, imag, slow):
+    block = slow // 2
+    half = block // 2
     results = [None] * block
     for parity in range(2):
         sign = 1.0 - 2.0 * parity
-        cos_part = [weighted([(1.0, real[k]), (sign, real[devices - k])]) for k in range(half)]
-        sin_part = [weighted([(1.0, imag[k]), (-sign, imag[devices - k])]) for k in range(half)]
+        cos_part = [weighted([(1.0, real[k]), (sign, real[block - k])]) for k in range(half)]
+        sin_part = [weighted([(1.0, imag[k]), (-sign, imag[block - k])]) for k in range(half)]
         for a in range(parity, block, 2):
             terms = [(circle(slow, a * k)[0], cos_part[k]) for k in range(half)]
             terms += [(circle(slow, a * k)[1], sin_part[k]) for k in range(1, half)]
             terms += [(circle(slow, a * half)[0], real[half]), (circle(slow, a * half)[1], imag[half])]
             results[a] = weighted(terms)
+    return results
+
+
+def complex_sum(pairs):
+    real, imag = None, None
+    for first, second, conjugate in pairs:
+        fast = first.shape[1] // 2
+        (a, b), (c, d) = ((x[:, :fast], x[:, fast:]) for x in (first, second))
+        one = a * c + b * d if conjugate else a * c - b * d
+        two = b * c - a * d if conjugate else -(a * d + b * c)
+        real, imag = (one, two) if real is None else (real + one, imag + two)
+    return jnp.concatenate([real, imag], axis=1)
+
+
+def convolve_kernel(signal_ref, high_ref, low_ref, turns_ref, *out_refs):
+    devices, stacked, fast = signal_ref.shape
+    group, block = stacked // 3, len(out_refs)
+    slow, count = 2 * block, block + 1
+    position = lax.axis_index("ctx")
+    first_half = position < block
+
+    def turn(which, k):
+        return turns_ref[which, k : k + 1, :], turns_ref[which, count + k : count + k + 1, :]
+
+    order = exchange_order(devices)
+    signal = [signal_ref[order.index(a)] for a in range(devices)]
+    halves = [slow_transform(signal[first : first + block], slow) for first in (0, block)]
+    rows = []
+    for k in range(count):
+        cos, sin = turn(0, k)
+        for real, imag in halves:
+            if k == 0:
+                turned = (real[k], jnp.zeros_like(real[k]))
+            elif imag[k] is None:
+                turned = (real[k] * cos, -(real[k] * sin))
+            else:
+                turned = (real[k] * cos + imag[k] * sin, imag[k] * cos - real[k] * sin)
+            rows.append(jnp.concatenate(turned, axis=1))
+    high, low = high_ref[...], low_ref[...]
+    spectrum = product(jnp.concatenate(rows, axis=0), high, low)
+    rows = []
+    for k in range(count):
+        parts = [spectrum[2 * k * stacked + i * group : 2 * k * stacked + (i + 1) * group] for i in range(6)]
+        gated, taps, grad, gated_late, taps_late, grad_late = parts
+        shift = 1.0 - 2.0 * (k % 2)
+        nothing = jnp.zeros_like(gated)
+        grad_near = jnp.where(first_half, weighted([(1.0, grad), (shift, grad_late)]), grad_late)
+        grad_far = jnp.where(first_half, grad_late, nothing)
+        gated_near = jnp.where(first_half, gated, weighted([(1.0, gated_late), (shift, gated)]))
+        gated_far = jnp.where(first_half, nothing, gated)
+        rows.append(complex_sum([(taps, gated_near, False), (taps_late, gated_far, False)]))
+        rows.append(complex_sum([(taps, grad_near, True), (taps_late, grad_far, True)]))
+        rows.append(complex_sum([(gated, grad_near, True), (gated_late, grad_far, True)]))
+    back = product(jnp.concatenate(rows, axis=0), high, low)
+    real, imag = [], []
+    for k in range(count):
+        cos, sin = turn(1, k)
+        row = back[k * stacked : (k + 1) * stacked]
+        real.append(row[:, :fast] * cos + row[:, fast:] * sin)
+        imag.append(row[:, fast:] * cos - row[:, :fast] * sin)
+    results = slow_inverse(real, imag, slow)
     for out_ref, result in zip(out_refs, by_partner(results, position % block), strict=True):
         out_ref[...] = result
 
@@ -387,7 +389,7 @@
         in_specs=[vmem] * 4,
         out_specs=[vmem] * block,
         compiler_params=params,
-    )(signals, *transform_tables(devices, block, fast, tap_scale))
+    )(signals, *transform_tables(block, fast, tap_scale))
     order = (3, 1, 2)
     results = list(results[:1]) + [lax.ppermute(results[x], "ctx", [(i, i ^ x) for i in range(devices)]) for x in order]
     return pl.pallas_call(
@@ -407,7 +409,7 @@
     devices = lax.axis_size("ctx")
     channels, fast = filter_raw.shape
     block = 4
-    if devices % block == 0 and devices <= 16 and channels % (16 * block) == 0 and fast % 128 == 0:
+    if devices == 2 * block and channels % (16 * block) == 0 and fast % 128 == 0:
         return by_channel(streams, filter_raw, grad_output, block)
     return by_residue(streams, filter_raw, grad_output)
 

time: 21.5 us -> 21.5 us (level)
  no operation moved by 1% of the time
where the time goes in v6:
time: 21.5 us; the launch traced here: 21.3 us
  blocking collectives  12.8 us (60%)
  starting transfers between devices  3.55 us (17%)
  Pallas kernels  2.13 us (10%)
  waiting for transfers between devices  2.1 us (10%)
  between operations  0.69 us (3%)
    all_to_all x1, blocking collectives, by_channel(): lax.all_to_all(signals, 'ctx', split_axis=0, concat_axis=0, axis_index_gr...  12.8 us
    ppermute x3, starting transfers between devices, by_channel(): lax.ppermute(results[x], 'ctx', [(i, i ^ x) for i in range(devices)])  3.55 us
    ppermute x3, waiting for transfers between devices, by_channel(): lax.ppermute(results[x], 'ctx', [(i, i ^ x) for i in range(devices)])  2.1 us
    pallas_call x1, Pallas kernels, by_channel(): pl.pallas_call(gate_kernel, out_shape=jax.ShapeDtypeStruct((devices, stac...  0.84 us
    pallas_call x1, Pallas kernels, by_channel(): pl.pallas_call(output_kernel, out_shape=(jax.ShapeDtypeStruct((channels,...  0.65 us
    pallas_call x1, Pallas kernels, by_channel(): pl.pallas_call(convolve_kernel, out_shape=[jax.ShapeDtypeStruct((stacked,...  0.63 us
  transfers between devices with their start and end apart: 3, of which 3 were waited for; matrix products, arithmetic and copies ran while one was open for 0% of the time, Pallas kernels for 0%

profile of v6, /device:TPU:0, one launch (start us, length us, event | category | flops | bytes accessed | tf_op | source)
XLA Modules:
  0.0 21.3 jit_solution(8431787489412343818)
XLA Ops:
  0.6 0.8 %shard_map.85 = f32[8,48,128]{2,1,0:T(8,128)S(1)} custom-call(bf16[3,64,128]{2,1,0:T(8,128)(2,1)} %streams_ref.1, f32[64,128]{1,0:T(8,128)} %filter_hbm.1, bf16[64,128]{1,0:T(8,128)(2,1)} %upstream_ref.1), custom_call_target="tpu_custom_call" | custom-call | tf_op jit(solution)/shard_map/pallas_call | solution.py:370
  1.5 0.0 copy-start.1
  1.5 0.0 copy-start.2
  1.5 0.0 copy-start.4
  1.5 12.8 %all_to_all.5.signal_ref = f32[8,48,128]{2,1,0:T(8,128)S(1)} all-to-all(f32[8,48,128]{2,1,0:T(8,128)S(1)} %shard_map.85), channel_id=1, replica_groups={{20,4,24,0,8,16,12,28},{21,5,25,1,9,17,13,29},{22,6,26,2,10,18,14,30},{..., dimensions={0} | all-to-all | bytes 393216 | tf_op jit(solution)/shard_map/all_to_all | solution.py:383
  14.3 0.0 copy-done.1
  14.3 0.0 copy-done.2
  14.3 0.0 copy-done.4
  14.3 0.0 copy-start
  14.3 0.0 copy-start.3
  14.3 0.6 %shard_map.86 = (f32[48,128]{1,0:T(8,128)S(1)}, f32[48,128]{1,0:T(8,128)S(1)}, f32[48,128]{1,0:T(8,128)S(1)}, f32[48,128]{1,0:T(8,128)S(1)}) custom-call(f32[8,48,128]{2,1,0:T(8,128)S(1)} %all_to_all.5.signal_ref, bf16[256,256]{1,0:T(8,128)(2,1)S(1)} %copy-done.2, bf16[256,256]{1,0:T(8,128)(2,1)S(1)} %copy-done.1, f32[2,10,128]{2,1,0:T(8,128)S(1)} %copy-done.4), custom_call_target="tpu_custom_call" | custom-call | tf_op jit(solution)/shard_map/pallas_call | solution.py:386
  15.0 1.6 %collective-permute-start = (f32[48,128]{1,0:T(8,128)S(1)}, f32[48,128]{1,0:T(8,128)S(1)}, u32[]{:S(2)}, u32[]{:S(2)}) collective-permute-start(f32[48,128]{1,0:T(8,128)S(1)} %get-tuple-element.8), channel_id=1, source_target_pairs={{0,12},{4,8},{8,4},{12,0},{16,28},{20,24},{24,20},{28,16},{1,13},{... | collective-permute-start | bytes 73736 | tf_op jit(solution)/shard_map/ppermute | solution.py:394
  16.6 0.2 collective-permute-start.1
  16.8 1.7 %collective-permute-start.2 = (f32[48,128]{1,0:T(8,128)S(1)}, f32[48,128]{1,0:T(8,128)S(1)}, u32[]{:S(2)}, u32[]{:S(2)}) collective-permute-start(f32[48,128]{1,0:T(8,128)S(1)} %get-tuple-element.10), channel_id=1, source_target_pairs={{0,8},{4,12},{8,0},{12,4},{16,24},{20,28},{24,16},{28,20},{1,9},{5... | collective-permute-start | bytes 73736 | tf_op jit(solution)/shard_map/ppermute | solution.py:394
  18.5 1.2 %collective-permute-done.refs_1_ = f32[48,128]{1,0:T(8,128)S(1)} collective-permute-done((f32[48,128]{1,0:T(8,128)S(1)}, f32[48,128]{1,0:T(8,128)S(1)}, u32[]{:S(2)}, u32[]{:S(2)}) %collective-permute-start) | collective-permute-done | bytes 24608 | tf_op jit(solution)/shard_map/ppermute | solution.py:394
  19.7 0.6 %collective-permute-done.1.refs_2_ = f32[48,128]{1,0:T(8,128)S(1)} collective-permute-done((f32[48,128]{1,0:T(8,128)S(1)}, f32[48,128]{1,0:T(8,128)S(1)}, u32[]{:S(2)}, u32[]{:S(2)}) %collective-permute-start.1) | collective-permute-done | bytes 24608 | tf_op jit(solution)/shard_map/ppermute | solution.py:394
  20.4 0.2 collective-permute-done.2.refs_3_
  20.6 0.0 copy-done
  20.6 0.0 copy-done.3
  20.6 0.7 %shard_map.87 = (bf16[64,128]{1,0:T(8,128)(2,1)}, bf16[3,64,128]{2,1,0:T(8,128)(2,1)}, f32[64,128]{1,0:T(8,128)}) custom-call(bf16[3,64,128]{2,1,0:T(8,128)(2,1)S(1)} %copy-done, bf16[64,128]{1,0:T(8,128)(2,1)S(1)} %copy-done.3, f32[48,128]{1,0:T(8,128)S(1)} %get-tuple-element.7.refs_0_, f32[48,128]{1,0:T(8,128)S(1)} %collective-permute-done.refs_1_, ...), custom_call_target="tpu_custom_call" | custom-call | tf_op jit(solution)/shard_map/pallas_call | solution.py:395
Async XLA Ops:
  1.5 12.8 %copy-start.1 = (bf16[256,256]{1,0:T(8,128)(2,1)S(1)}, bf16[256,256]{1,0:T(8,128)(2,1)}, u32[]{:S(2)}) copy-start(bf16[256,256]{1,0:T(8,128)(2,1)} %constant.7.clone.low_ref) | copy-start | bytes 393220
  1.5 12.8 %copy-start.2 = (bf16[256,256]{1,0:T(8,128)(2,1)S(1)}, bf16[256,256]{1,0:T(8,128)(2,1)}, u32[]{:S(2)}) copy-start(bf16[256,256]{1,0:T(8,128)(2,1)} %constant.6.clone.high_ref) | copy-start | bytes 393220
  1.5 12.8 %copy-start.4 = (f32[2,10,128]{2,1,0:T(8,128)S(1)}, f32[2,10,128]{2,1,0:T(8,128)}, u32[]{:S(2)}) copy-start(f32[2,10,128]{2,1,0:T(8,128)} %constant.8.clone.turns_ref) | copy-start | bytes 30724
  14.3 6.3 %copy-start = (bf16[3,64,128]{2,1,0:T(8,128)(2,1)S(1)}, bf16[3,64,128]{2,1,0:T(8,128)(2,1)}, u32[]{:S(2)}) copy-start(bf16[3,64,128]{2,1,0:T(8,128)(2,1)} %streams_ref.1) | copy-start | bytes 147460
  14.3 6.3 %copy-start.3 = (bf16[64,128]{1,0:T(8,128)(2,1)S(1)}, bf16[64,128]{1,0:T(8,128)(2,1)}, u32[]{:S(2)}) copy-start(bf16[64,128]{1,0:T(8,128)(2,1)} %upstream_ref.1) | copy-start | bytes 49156
  15.0 4.8 %collective-permute-start = (f32[48,128]{1,0:T(8,128)S(1)}, f32[48,128]{1,0:T(8,128)S(1)}, u32[]{:S(2)}, u32[]{:S(2)}) collective-permute-start(f32[48,128]{1,0:T(8,128)S(1)} %get-tuple-element.8), channel_id=1, source_target_pairs={{0,12},{4,8},{8,4},{12,0},{16,28},{20,24},{24,20},{28,16},{1,13},{... | collective-permute-start | bytes 73736 | tf_op jit(solution)/shard_map/ppermute | solution.py:394
  16.6 3.8 %collective-permute-start.1 = (f32[48,128]{1,0:T(8,128)S(1)}, f32[48,128]{1,0:T(8,128)S(1)}, u32[]{:S(2)}, u32[]{:S(2)}) collective-permute-start(f32[48,128]{1,0:T(8,128)S(1)} %get-tuple-element.9), channel_id=1, source_target_pairs={{0,4},{4,0},{8,12},{12,8},{16,20},{20,16},{24,28},{28,24},{1,5},{5... | collective-permute-start | bytes 73736 | tf_op jit(solution)/shard_map/ppermute | solution.py:394
  16.8 3.8 %collective-permute-start.2 = (f32[48,128]{1,0:T(8,128)S(1)}, f32[48,128]{1,0:T(8,128)S(1)}, u32[]{:S(2)}, u32[]{:S(2)}) collective-permute-start(f32[48,128]{1,0:T(8,128)S(1)} %get-tuple-element.10), channel_id=1, source_target_pairs={{0,8},{4,12},{8,0},{12,4},{16,24},{20,28},{24,16},{28,20},{1,9},{5... | collective-permute-start | bytes 73736 | tf_op jit(solution)/shard_map/ppermute | solution.py:394

commit v7 on v6

--- a/solution.py
+++ b/solution.py
@@ -223,7 +223,7 @@
 
 
 def exchange_order(devices):
-    return [5, 1, 6, 0, 2, 4, 3, 7] if devices == 8 else list(range(devices))
+    return [5, 1, 6, 4, 2, 0, 7, 3] if devices == 8 else list(range(devices))
 
 
 def gate_kernel(streams_hbm, filter_hbm, upstream_hbm, out_ref, streams_ref, filter_ref, upstream_ref, arrived):
@@ -350,7 +350,7 @@
     channels, _ = filter_grad_ref.shape
     block = len(back_refs)
     group = channels // block
-    parts = by_partner([back_refs[k][...] for k in [0, 2, 3, 1]], lax.axis_index("ctx") % block)
+    parts = by_partner([back_refs[k][...] for k in [0, 3, 2, 1]], lax.axis_index("ctx") % block)
     long_conv = jnp.concatenate([part[:group] for part in parts], axis=0)
     grad_gated = jnp.concatenate([part[group : 2 * group] for part in parts], axis=0)
     filter_grad_ref[...] = jnp.concatenate([part[2 * group :] for part in parts], axis=0)
@@ -390,7 +390,7 @@
         out_specs=[vmem] * block,
         compiler_params=params,
     )(signals, *transform_tables(block, fast, tap_scale))
-    order = (3, 1, 2)
+    order = (3, 2, 1)
     results = list(results[:1]) + [lax.ppermute(results[x], "ctx", [(i, i ^ x) for i in range(devices)]) for x in order]
     return pl.pallas_call(
         output_kernel,

time: 21.5 us -> 21.3 us (level)
  blocking collectives: 12.8 us -> 11.8 us
  waiting for transfers between devices: 2.1 us -> 2.86 us
    all_to_all x1, blocking collectives: 12.8 us -> 11.8 us  [by_channel(): lax.all_to_all(signals, 'ctx', split_axis=0, concat_axis=0, axis_index_gr...]
    ppermute x3, waiting for transfers between devices: 2.1 us -> 2.86 us  [by_channel(): lax.ppermute(results[x], 'ctx', [(i, i ^ x) for i in range(devices)])]
  transfers between devices with their start and end apart: 3 -> 3, of which waited for: 3 -> 2; matrix products, arithmetic and copies ran while one was open for 0% -> 0% of each run, Pallas kernels for 0% -> 0%
where the time goes in v7:
time: 21.3 us; the launch traced here: 21.1 us
  blocking collectives  11.8 us (55%)
  starting transfers between devices  3.55 us (17%)
  waiting for transfers between devices  2.86 us (13%)
  Pallas kernels  2.14 us (10%)
  between operations  0.7 us (3%)
    all_to_all x1, blocking collectives, by_channel(): lax.all_to_all(signals, 'ctx', split_axis=0, concat_axis=0, axis_index_gr...  11.8 us
    ppermute x3, starting transfers between devices, by_channel(): lax.ppermute(results[x], 'ctx', [(i, i ^ x) for i in range(devices)])  3.55 us
    ppermute x3, waiting for transfers between devices, by_channel(): lax.ppermute(results[x], 'ctx', [(i, i ^ x) for i in range(devices)])  2.86 us
    pallas_call x1, Pallas kernels, by_channel(): pl.pallas_call(gate_kernel, out_shape=jax.ShapeDtypeStruct((devices, stac...  0.84 us
    pallas_call x1, Pallas kernels, by_channel(): pl.pallas_call(output_kernel, out_shape=(jax.ShapeDtypeStruct((channels,...  0.66 us
    pallas_call x1, Pallas kernels, by_channel(): pl.pallas_call(convolve_kernel, out_shape=[jax.ShapeDtypeStruct((stacked,...  0.63 us
  transfers between devices with their start and end apart: 3, of which 2 were waited for; matrix products, arithmetic and copies ran while one was open for 0% of the time, Pallas kernels for 0%

profile of v7, /device:TPU:0, one launch (start us, length us, event | category | flops | bytes accessed | tf_op | source)
XLA Modules:
  0.0 21.1 jit_solution(14313289772612487830)
XLA Ops:
  0.6 0.8 %shard_map.85 = f32[8,48,128]{2,1,0:T(8,128)S(1)} custom-call(bf16[3,64,128]{2,1,0:T(8,128)(2,1)} %streams_ref.1, f32[64,128]{1,0:T(8,128)} %filter_hbm.1, bf16[64,128]{1,0:T(8,128)(2,1)} %upstream_ref.1), custom_call_target="tpu_custom_call" | custom-call | tf_op jit(solution)/shard_map/pallas_call | solution.py:370
  1.5 0.0 copy-start.1
  1.5 0.0 copy-start.2
  1.5 0.0 copy-start.4
  1.5 11.8 %all_to_all.5.signal_ref = f32[8,48,128]{2,1,0:T(8,128)S(1)} all-to-all(f32[8,48,128]{2,1,0:T(8,128)S(1)} %shard_map.85), channel_id=1, replica_groups={{20,4,24,16,8,0,28,12},{21,5,25,17,9,1,29,13},{22,6,26,18,10,2,30,14},{..., dimensions={0} | all-to-all | bytes 393216 | tf_op jit(solution)/shard_map/all_to_all | solution.py:383
  13.4 0.0 copy-done.1
  13.4 0.0 copy-done.2
  13.4 0.0 copy-done.4
  13.4 0.0 copy-start
  13.4 0.0 copy-start.3
  13.4 0.6 %shard_map.86 = (f32[48,128]{1,0:T(8,128)S(1)}, f32[48,128]{1,0:T(8,128)S(1)}, f32[48,128]{1,0:T(8,128)S(1)}, f32[48,128]{1,0:T(8,128)S(1)}) custom-call(f32[8,48,128]{2,1,0:T(8,128)S(1)} %all_to_all.5.signal_ref, bf16[256,256]{1,0:T(8,128)(2,1)S(1)} %copy-done.2, bf16[256,256]{1,0:T(8,128)(2,1)S(1)} %copy-done.1, f32[2,10,128]{2,1,0:T(8,128)S(1)} %copy-done.4), custom_call_target="tpu_custom_call" | custom-call | tf_op jit(solution)/shard_map/pallas_call | solution.py:386
  14.0 2.6 %collective-permute-start = (f32[48,128]{1,0:T(8,128)S(1)}, f32[48,128]{1,0:T(8,128)S(1)}, u32[]{:S(2)}, u32[]{:S(2)}) collective-permute-start(f32[48,128]{1,0:T(8,128)S(1)} %get-tuple-element.8), channel_id=1, source_target_pairs={{0,12},{4,8},{8,4},{12,0},{16,28},{20,24},{24,20},{28,16},{1,13},{... | collective-permute-start | bytes 73736 | tf_op jit(solution)/shard_map/ppermute | solution.py:394
  16.6 0.0 collective-permute-start.1
  16.6 1.0 %collective-permute-start.2 = (f32[48,128]{1,0:T(8,128)S(1)}, f32[48,128]{1,0:T(8,128)S(1)}, u32[]{:S(2)}, u32[]{:S(2)}) collective-permute-start(f32[48,128]{1,0:T(8,128)S(1)} %get-tuple-element.10), channel_id=1, source_target_pairs={{0,4},{4,0},{8,12},{12,8},{16,20},{20,16},{24,28},{28,24},{1,5},{5... | collective-permute-start | bytes 73736 | tf_op jit(solution)/shard_map/ppermute | solution.py:394
  17.6 1.2 %collective-permute-done.refs_1_ = f32[48,128]{1,0:T(8,128)S(1)} collective-permute-done((f32[48,128]{1,0:T(8,128)S(1)}, f32[48,128]{1,0:T(8,128)S(1)}, u32[]{:S(2)}, u32[]{:S(2)}) %collective-permute-start) | collective-permute-done | bytes 24608 | tf_op jit(solution)/shard_map/ppermute | solution.py:394
  18.8 1.6 %collective-permute-done.1.refs_2_ = f32[48,128]{1,0:T(8,128)S(1)} collective-permute-done((f32[48,128]{1,0:T(8,128)S(1)}, f32[48,128]{1,0:T(8,128)S(1)}, u32[]{:S(2)}, u32[]{:S(2)}) %collective-permute-start.1) | collective-permute-done | bytes 24608 | tf_op jit(solution)/shard_map/ppermute | solution.py:394
  20.5 0.0 collective-permute-done.2.refs_3_
  20.5 0.0 copy-done
  20.5 0.0 copy-done.3
  20.5 0.7 %shard_map.87 = (bf16[64,128]{1,0:T(8,128)(2,1)}, bf16[3,64,128]{2,1,0:T(8,128)(2,1)}, f32[64,128]{1,0:T(8,128)}) custom-call(bf16[3,64,128]{2,1,0:T(8,128)(2,1)S(1)} %copy-done, bf16[64,128]{1,0:T(8,128)(2,1)S(1)} %copy-done.3, f32[48,128]{1,0:T(8,128)S(1)} %get-tuple-element.7.refs_0_, f32[48,128]{1,0:T(8,128)S(1)} %collective-permute-done.refs_1_, ...), custom_call_target="tpu_custom_call" | custom-call | tf_op jit(solution)/shard_map/pallas_call | solution.py:395
Async XLA Ops:
  1.5 11.9 %copy-start.1 = (bf16[256,256]{1,0:T(8,128)(2,1)S(1)}, bf16[256,256]{1,0:T(8,128)(2,1)}, u32[]{:S(2)}) copy-start(bf16[256,256]{1,0:T(8,128)(2,1)} %constant.7.clone.low_ref) | copy-start | bytes 393220
  1.5 11.9 %copy-start.2 = (bf16[256,256]{1,0:T(8,128)(2,1)S(1)}, bf16[256,256]{1,0:T(8,128)(2,1)}, u32[]{:S(2)}) copy-start(bf16[256,256]{1,0:T(8,128)(2,1)} %constant.6.clone.high_ref) | copy-start | bytes 393220
  1.5 11.9 %copy-start.4 = (f32[2,10,128]{2,1,0:T(8,128)S(1)}, f32[2,10,128]{2,1,0:T(8,128)}, u32[]{:S(2)}) copy-start(f32[2,10,128]{2,1,0:T(8,128)} %constant.8.clone.turns_ref) | copy-start | bytes 30724
  13.4 7.1 %copy-start = (bf16[3,64,128]{2,1,0:T(8,128)(2,1)S(1)}, bf16[3,64,128]{2,1,0:T(8,128)(2,1)}, u32[]{:S(2)}) copy-start(bf16[3,64,128]{2,1,0:T(8,128)(2,1)} %streams_ref.1) | copy-start | bytes 147460
  13.4 7.1 %copy-start.3 = (bf16[64,128]{1,0:T(8,128)(2,1)S(1)}, bf16[64,128]{1,0:T(8,128)(2,1)}, u32[]{:S(2)}) copy-start(bf16[64,128]{1,0:T(8,128)(2,1)} %upstream_ref.1) | copy-start | bytes 49156
  14.0 4.8 %collective-permute-start = (f32[48,128]{1,0:T(8,128)S(1)}, f32[48,128]{1,0:T(8,128)S(1)}, u32[]{:S(2)}, u32[]{:S(2)}) collective-permute-start(f32[48,128]{1,0:T(8,128)S(1)} %get-tuple-element.8), channel_id=1, source_target_pairs={{0,12},{4,8},{8,4},{12,0},{16,28},{20,24},{24,20},{28,16},{1,13},{... | collective-permute-start | bytes 73736 | tf_op jit(solution)/shard_map/ppermute | solution.py:394
  16.6 3.8 %collective-permute-start.1 = (f32[48,128]{1,0:T(8,128)S(1)}, f32[48,128]{1,0:T(8,128)S(1)}, u32[]{:S(2)}, u32[]{:S(2)}) collective-permute-start(f32[48,128]{1,0:T(8,128)S(1)} %get-tuple-element.9), channel_id=1, source_target_pairs={{0,8},{4,12},{8,0},{12,4},{16,24},{20,28},{24,16},{28,20},{1,9},{5... | collective-permute-start | bytes 73736 | tf_op jit(solution)/shard_map/ppermute | solution.py:394
  16.6 3.8 %collective-permute-start.2 = (f32[48,128]{1,0:T(8,128)S(1)}, f32[48,128]{1,0:T(8,128)S(1)}, u32[]{:S(2)}, u32[]{:S(2)}) collective-permute-start(f32[48,128]{1,0:T(8,128)S(1)} %get-tuple-element.10), channel_id=1, source_target_pairs={{0,4},{4,0},{8,12},{12,8},{16,20},{20,16},{24,28},{28,24},{1,5},{5... | collective-permute-start | bytes 73736 | tf_op jit(solution)/shard_map/ppermute | solution.py:394
